TPU v7x, 32 devices: a whole 2x2x4 slice. The times are simulated.
32 devices in a mesh: group: 2 (over y), lat: 4 (over z), lon: 2 (over x), sub: 2 (over core).
Axes of the slice: x: 2, y: 2, z: 4, core: 2. Of those that a mesh axis runs over, the one named last changes fastest.
Arguments:
- grid_latent: bfloat16 [8192, 512], P(('group', 'lat', 'lon', 'sub')), parts along dimension 0, may hold values from -6 to 6
- grid_band: int32 [8192, 1], P(('group', 'lat', 'lon', 'sub')), parts along dimension 0, may hold values from 0 to 3; in each aligned block of 256 rows (0 to 255, 256 to 511, ...) at most 128 rows name the same one
- edge_rows: int32 [8192, 2], P(('group', 'lat', 'lon', 'sub')), parts along dimension 0, may hold values from 0 to 63
- mesh_latent: bfloat16 [1024, 512], P(('group', 'lat', 'lon')), parts along dimension 0, may hold values from -6 to 6
- mesh_slots: int32 [1024, 8], P(('group', 'lat', 'lon'), 'sub'), parts along dimension 0, may hold values from 0 to 191, as said below
- send_rows: int32 [16, 8, 16], P(('group', 'lat', 'lon')), parts along dimension 0, may hold values from 0 to 63
- enc_send: bfloat16 [512, 512], replicated, may hold values from -0.25 to 0.25
- enc_recv: bfloat16 [512, 512], replicated, may hold values from -0.25 to 0.25
- enc_edge: bfloat16 [512, 512], replicated, may hold values from -0.25 to 0.25
- bias_grid: float32 [512], replicated, may hold values from -4 to 4
- node_gain: float32 [512], replicated, may hold values from 0.1 to 1.9
- proc_send: bfloat16 [512, 512], replicated, may hold values from -0.25 to 0.25
- proc_recv: bfloat16 [512, 512], replicated, may hold values from -0.25 to 0.25
- proc_edge: bfloat16 [512, 512], replicated, may hold values from -0.25 to 0.25
- bias_mesh: float32 [512], replicated, may hold values from -4 to 4
- mesh_gain: float32 [512], replicated, may hold values from 0.1 to 1.9
- cotangent: bfloat16 [1024, 512], P(('group', 'lat', 'lon')), parts along dimension 0, may hold values from -6 to 6
Outputs:
- mesh_out: bfloat16 [1024, 512], P(('group', 'lat', 'lon')), parts along dimension 0
- mesh_grad: bfloat16 [1024, 512], P(('group', 'lat', 'lon')), parts along dimension 0
- grid_grad: bfloat16 [8192, 512], P(('group', 'lat', 'lon', 'sub')), parts along dimension 0
There are 2 independent parts, one for each index of `group`. A program takes and returns all parts, laid end to end along the dimension named above; an argument that names none is the same for every part. Nothing has to cross between parts.
Inputs may be any that keep to these rules, and one draw needn't show every extreme that they name: `grid_band`: among the grid nodes of one device at most 128 name the same band, and in every draw some device's nodes name one band exactly 128 times. `mesh_slots`: A slot at or above 64 never refers to a band outside 0 to 3.
All inputs are finite; a program needn't handle non-finite values.
Results may differ from a plain program's by a relative error of at most 0.014.
Values may be sent and summed in bfloat16 or wider, within the bound.
A program may use at most 64 MiB of HBM per device.

v0:
```python
import jax
import jax.numpy as jnp
from jax import lax
from jax.sharding import PartitionSpec as P

EPS = 1e-05
DIRECTIONS = ((-1, -1), (-1, 0), (-1, 1), (0, -1), (0, 1), (1, -1), (1, 0), (1, 1))


def passed_along(shard, axis, by):
    devices = lax.axis_size(axis)
    return lax.ppermute(shard, axis, [(i, (i + by) % devices) for i in range(devices)])


def passed_along_2(block, axis, distance):
    devices = range(lax.axis_size(axis))
    route = [(i - distance, i) for i in devices if i - distance in devices]
    return lax.ppermute(block, axis, route)


def as_sent(shard):
    return jax.tree.map(lambda a: a.astype(jnp.bfloat16) if a.dtype == jnp.float32 else a, shard)


def layer_norm(value):
    centred = value - jnp.mean(value, -1, keepdims=True)
    return centred * lax.rsqrt(jnp.mean(centred * centred, -1, keepdims=True) + EPS)


def norm_back(value, upstream):
    centred = value - jnp.mean(value, -1, keepdims=True)
    inverse = lax.rsqrt(jnp.mean(centred * centred, -1, keepdims=True) + EPS)
    normed = centred * inverse
    inner = jnp.mean(upstream * normed, -1, keepdims=True)
    return (upstream - jnp.mean(upstream, -1, keepdims=True) - normed * inner) * inverse


def silu_slope(value):
    sigma = jax.nn.sigmoid(value)
    return sigma * (1.0 + value * (1.0 - sigma))


def dot_plain(left, right):
    return jnp.dot(left, right, preferred_element_type=jnp.float32)


def dot_trans(left, right):
    return lax.dot_general(
        left, right, (((1,), (1,)), ((), ())), preferred_element_type=jnp.float32
    )


def pool_rows(row_ids, values, count):
    matches = jnp.arange(count, dtype=jnp.int32)[:, None] == row_ids[None, :]
    if values.dtype == jnp.bfloat16:
        return jnp.dot(matches.astype(jnp.bfloat16), values, preferred_element_type=jnp.float32)
    return jnp.dot(
        matches.astype(jnp.float32),
        values,
        preferred_element_type=jnp.float32,
        precision=lax.Precision.HIGHEST,
    )


def spread_out(blocks):
    pieces = [blocks[d] for d in range(8)]
    for d in range(8):
        lat_by, lon_by = DIRECTIONS[d]
        if lon_by != 0:
            pieces[d] = passed_along(pieces[d], "lon", lon_by)
        if lat_by != 0:
            pieces[d] = passed_along_2(pieces[d], "lat", lat_by)
    return jnp.stack(pieces)


def spread_back(blocks):
    pieces = [blocks[d] for d in range(8)]
    for d in range(8):
        lat_by, lon_by = DIRECTIONS[d]
        if lat_by != 0:
            pieces[d] = passed_along_2(pieces[d].astype(jnp.bfloat16), "lat", -lat_by).astype(
                jnp.float32
            )
        if lon_by != 0:
            pieces[d] = passed_along(as_sent(pieces[d]), "lon", -lon_by)
    return jnp.stack(pieces)


def on_device(
    grid_latent,
    grid_band,
    edge_rows,
    mesh_latent,
    mesh_slots,
    send_rows,
    enc_send,
    enc_recv,
    enc_edge,
    bias_grid,
    node_gain,
    proc_send,
    proc_recv,
    proc_edge,
    bias_mesh,
    mesh_gain,
    cotangent,
):
    bands = lax.axis_size("lat")
    local_rows = grid_latent.shape[0]
    mesh_rows = mesh_latent.shape[0]
    width = grid_latent.shape[1]
    fanout = edge_rows.shape[1]
    capacity = 2 * local_rows // bands
    slot_count = bands * capacity
    band_of = grid_band[:, 0]
    member = (band_of[:, None] == jnp.arange(bands, dtype=jnp.int32)[None, :]).astype(jnp.int32)
    ranked = jnp.sum((jnp.cumsum(member, 0) - 1) * member, 1)
    position = band_of * capacity + ranked
    target_out = jnp.full((slot_count, fanout), -1, jnp.int32).at[position].set(edge_rows)
    outgoing = jnp.zeros((slot_count, width), jnp.bfloat16).at[position].set(grid_latent)
    arrived = lax.all_to_all(outgoing, "lat", split_axis=0, concat_axis=0, tiled=True)
    arrived_targets = lax.all_to_all(target_out, "lat", split_axis=0, concat_axis=0, tiled=True)
    proj_slots = dot_plain(arrived, enc_send).astype(jnp.bfloat16)
    valid = (arrived_targets >= 0).astype(jnp.float32)[:, :, None]
    safe_rows = jnp.maximum(arrived_targets, 0)
    flat_targets = arrived_targets.reshape(-1)
    proj_mesh = dot_plain(mesh_latent, enc_recv).astype(jnp.bfloat16)
    pre_grid = (
        proj_slots.astype(jnp.float32)[:, None, :]
        + proj_mesh[safe_rows].astype(jnp.float32)
        + bias_grid
    )
    hid_grid = jax.nn.silu(pre_grid).astype(jnp.bfloat16)
    z_grid = jnp.einsum("skd,de->ske", hid_grid, enc_edge, preferred_element_type=jnp.float32)
    messages = (layer_norm(z_grid) * valid).reshape(-1, width)
    agg_local = pool_rows(flat_targets, messages, mesh_rows)
    agg_grid = lax.psum(agg_local, "sub")
    mesh_mid = (mesh_latent.astype(jnp.float32) + layer_norm(agg_grid) * node_gain).astype(
        jnp.bfloat16
    )
    send_mesh = dot_plain(mesh_mid, proc_send).astype(jnp.bfloat16)
    recv_mesh = dot_plain(mesh_mid, proc_recv).astype(jnp.bfloat16)
    own_lists = send_rows[0]
    boundary = spread_out(send_mesh[own_lists])
    table = jnp.concatenate([send_mesh, boundary.reshape(-1, width)], 0)
    table_rows = table.shape[0]
    pre_mesh = (
        table[mesh_slots].astype(jnp.float32)
        + recv_mesh.astype(jnp.float32)[:, None, :]
        + bias_mesh
    )
    hid_mesh = jax.nn.silu(pre_mesh).astype(jnp.bfloat16)
    z_mesh = jnp.einsum("mkd,de->mke", hid_mesh, proc_edge, preferred_element_type=jnp.float32)
    agg_mesh = lax.psum(jnp.sum(layer_norm(z_mesh), 1), "sub")
    mesh_out = (mesh_mid.astype(jnp.float32) + layer_norm(agg_mesh) * mesh_gain).astype(
        jnp.bfloat16
    )
    upstream = cotangent.astype(jnp.float32)
    d_agg_mesh = norm_back(agg_mesh, upstream * mesh_gain)
    d_z_mesh = norm_back(z_mesh, d_agg_mesh[:, None, :]).astype(jnp.bfloat16)
    d_hid_mesh = jnp.einsum("mke,de->mkd", d_z_mesh, proc_edge, preferred_element_type=jnp.float32)
    d_pre_rounded = (d_hid_mesh * silu_slope(pre_mesh)).astype(jnp.bfloat16)
    d_table_local = pool_rows(mesh_slots.reshape(-1), d_pre_rounded.reshape(-1, width), table_rows)
    d_recv_local = jnp.sum(d_pre_rounded.astype(jnp.float32), 1)
    d_table, d_recv = lax.psum((d_table_local, d_recv_local), "sub")
    returned = spread_back(d_table[mesh_rows:].reshape(8, -1, width))
    d_send = d_table[:mesh_rows] + pool_rows(
        own_lists.reshape(-1), returned.reshape(-1, width), mesh_rows
    )
    d_mid = (
        upstream
        + dot_trans(d_send.astype(jnp.bfloat16), proc_send)
        + dot_trans(d_recv.astype(jnp.bfloat16), proc_recv)
    )
    d_agg_grid = norm_back(agg_grid, d_mid * node_gain)
    d_z_grid = (norm_back(z_grid, d_agg_grid[safe_rows]) * valid).astype(jnp.bfloat16)
    d_hid_grid = jnp.einsum("ske,de->skd", d_z_grid, enc_edge, preferred_element_type=jnp.float32)
    d_pre_grid = (d_hid_grid * silu_slope(pre_grid)).astype(jnp.bfloat16)
    d_proj_local = pool_rows(flat_targets, d_pre_grid.reshape(-1, width), mesh_rows)
    d_proj_mesh = lax.psum(d_proj_local.astype(jnp.bfloat16), "sub")
    mesh_grad = (d_mid + dot_trans(d_proj_mesh, enc_recv)).astype(jnp.bfloat16)
    d_proj_slots = jnp.sum(d_pre_grid.astype(jnp.float32), 1).astype(jnp.bfloat16)
    back_payload = dot_trans(d_proj_slots, enc_send).astype(jnp.bfloat16)
    came_back = lax.all_to_all(back_payload, "lat", split_axis=0, concat_axis=0, tiled=True)
    mine = came_back[position]
    return (mesh_out, mesh_grad, mine)


def solution(mesh):
    placed = (
        P(("group", "lat", "lon", "sub"), None),
        P(("group", "lat", "lon", "sub"), None),
        P(("group", "lat", "lon", "sub"), None),
        P(("group", "lat", "lon"), None),
        P(("group", "lat", "lon"), "sub"),
        P(("group", "lat", "lon"), None, None),
        P(),
        P(),
        P(),
        P(),
        P(),
        P(),
        P(),
        P(),
        P(),
        P(),
        P(("group", "lat", "lon"), None),
    )
    return jax.shard_map(
        on_device,
        mesh=mesh,
        in_specs=placed,
        out_specs=(
            P(("group", "lat", "lon"), None),
            P(("group", "lat", "lon"), None),
            P(("group", "lat", "lon", "sub"), None),
        ),
        check_vma=False,
    )
```

profile of v0, /device:TPU:0, one launch (start us, length us, event | category | flops | bytes accessed | tf_op | source)
XLA Modules:
  0.0 260.5 jit_solution(9419110628624042629)
XLA Ops:
  13.7 6.3 %all-to-all-start = ((s32[4,128,2]{1,2,0:T(2,128)}), s32[4,128,2]{1,2,0:T(2,128)S(1)}, u32[]{:S(2)}, u32[]{:S(2)}) async-start(s32[4,128,2]{1,2,0:T(2,128)} %copy.39), calls=%async_computation | async-start | bytes 8192 | tf_op jit(solution)/shard_map/all_to_all | solution.py:122
  21.3 2.7 %scatter_custom_fusion.1 = bf16[512,512]{1,0:T(8,128)(2,1)} fusion(s32[256]{0:T(256)S(1)} %bitcast.112, bf16[256,512]{1,0:T(8,128)(2,1)} %param.17, bf16[]{:T(256)} %constant.54.clone.1), kind=kCustom, calls=%fused_computation.61 | custom fusion | bytes 524800 | tf_op jit(solution)/shard_map/scatter | solution.py:120
  25.6 3.5 %all-to-all-start.1 = ((bf16[4,128,512]{2,1,0:T(8,128)(2,1)}), bf16[4,128,512]{2,1,0:T(8,128)(2,1)S(1)}, u32[]{:S(2)}, u32[]{:S(2)}) async-start(bf16[4,128,512]{2,1,0:T(8,128)(2,1)} %bitcast.7), calls=%async_computation.1 | async-start | bytes 1048576 | tf_op jit(solution)/shard_map/all_to_all | solution.py:121
  30.0 4.0 %gather_fusion = bf16[1024,512]{1,0:T(8,128)(2,1)S(1)} fusion(bf16[64,512]{1,0:T(8,128)(2,1)S(1)} %convolution_convert_fusion.5, s32[1024]{0:T(1024)S(1)} %get-tuple-element.36), kind=kCustom, calls=%fused_computation | custom fusion | bytes 2101248 | tf_op jit(solution)/shard_map/gather | solution.py:130
  36.4 6.6 %all-to-all-done.1 = bf16[4,128,512]{2,1,0:T(8,128)(2,1)S(1)} async-done(((bf16[4,128,512]{2,1,0:T(8,128)(2,1)}), bf16[4,128,512]{2,1,0:T(8,128)(2,1)S(1)}, u32[]{:S(2)}, u32[]{:S(2)}) %all-to-all-start.1) | async-done | bytes 524320 | tf_op jit(solution)/shard_map/all_to_all | solution.py:121
  46.5 2.9 %copy.43 = f32[512,2,512]{2,1,0:T(2,128)} copy(f32[512,2,512]{2,0,1:T(8,128)S(1)} %fusion.1) | data formatting | bytes 4194304 | tf_op jit(solution)/shard_map/mul | solution.py:135
  49.4 3.7 %reshape.215 = f32[1024,512]{1,0:T(8,128)} reshape(f32[512,2,512]{2,1,0:T(2,128)} %copy.43) | data formatting | bytes 4194304 | tf_op jit(solution)/shard_map/reshape | solution.py:135
  53.2 3.2 %fusion.29 = f32[64,512]{1,0:T(8,128)} fusion(f32[1024,512]{1,0:T(8,128)} %reshape.215, s32[1024]{0:T(1024)S(1)} %eq.86), kind=kOutput, calls=%fused_computation.64 | convolution fusion | flops 402718720 | bytes 2232320 | tf_op jit(solution)/shard_map/dot_general | solution.py:57
  56.6 17.0 %all-reduce.6.cloned.1.call-done = f32[64,512]{1,0:T(8,128)} async-done(((f32[64,512]{1,0:T(8,128)}), f32[64,512]{1,0:T(8,128)}) %all-reduce.6.cloned.1.call-update) | async-done | bytes 131088 | tf_op jit(solution)/shard_map/psum | solution.py:137
  80.0 3.6 %collective-permute-start.9 = (bf16[16,512]{1,0:T(8,128)(2,1)S(1)}, bf16[16,512]{1,0:T(8,128)(2,1)S(1)}, u32[]{:S(2)}, u32[]{:S(2)}) collective-permute-start(bf16[16,512]{1,0:T(8,128)(2,1)S(1)} %get-tuple-element.19), channel_id=1, source_target_pairs={{0,4},{4,8},{8,12},{1,5},{5,9},{9,13},{2,6},{6,10},{10,14},{3,7},{... | collective-permute-start | bytes 49160 | tf_op jit(solution)/shard_map/ppermute | solution.py:18
  94.2 2.8 %collective-permute-done.2 = bf16[16,512]{1,0:T(8,128)(2,1)S(1)} collective-permute-done((bf16[16,512]{1,0:T(8,128)(2,1)S(1)}, bf16[16,512]{1,0:T(8,128)(2,1)S(1)}, u32[]{:S(2)}, u32[]{:S(2)}) %collective-permute-start.2) | collective-permute-done | bytes 16416 | tf_op jit(solution)/shard_map/ppermute | solution.py:18
  99.8 4.5 %collective-permute-start.11 = (bf16[16,512]{1,0:T(8,128)(2,1)S(1)}, bf16[16,512]{1,0:T(8,128)(2,1)S(1)}, u32[]{:S(2)}, u32[]{:S(2)}) collective-permute-start(bf16[16,512]{1,0:T(8,128)(2,1)S(1)} %collective-permute-done.10), channel_id=1, source_target_pairs={{0,4},{4,8},{8,12},{1,5},{5,9},{9,13},{2,6},{6,10},{10,14},{3,7},{... | collective-permute-start | bytes 49160 | tf_op jit(solution)/shard_map/ppermute | solution.py:18
  104.3 3.6 %collective-permute-start.8 = (bf16[16,512]{1,0:T(8,128)(2,1)S(1)}, bf16[16,512]{1,0:T(8,128)(2,1)S(1)}, u32[]{:S(2)}, u32[]{:S(2)}) collective-permute-start(bf16[16,512]{1,0:T(8,128)(2,1)S(1)} %collective-permute-done.7), channel_id=1, source_target_pairs={{0,4},{4,8},{8,12},{1,5},{5,9},{9,13},{2,6},{6,10},{10,14},{3,7},{... | collective-permute-start | bytes 49160 | tf_op jit(solution)/shard_map/ppermute | solution.py:18
  114.4 17.7 %all-reduce.8.cloned.1.call-done = f32[64,512]{1,0:T(8,128)} async-done(((f32[64,512]{1,0:T(8,128)}), f32[64,512]{1,0:T(8,128)}) %all-reduce.8.cloned.1.call-update) | async-done | bytes 131088 | tf_op jit(solution)/shard_map/psum | solution.py:154
  144.6 19.8 %all-reduce.10.cloned.1.call-done = f32[192,512]{1,0:T(8,128)} async-done(((f32[192,512]{1,0:T(8,128)}), f32[192,512]{1,0:T(8,128)}) %all-reduce.10.cloned.1.call-update) | async-done | bytes 393232 | tf_op jit(solution)/shard_map/psum | solution.py:165
  165.5 4.3 %collective-permute-start.12 = (bf16[16,512]{1,0:T(8,128)(2,1)S(1)}, bf16[16,512]{1,0:T(8,128)(2,1)}, u32[]{:S(2)}, u32[]{:S(2)}) collective-permute-start(bf16[16,512]{1,0:T(8,128)(2,1)S(1)} %get-tuple-element.16), channel_id=1, source_target_pairs={{0,4},{4,8},{8,12},{1,5},{5,9},{9,13},{2,6},{6,10},{10,14},{3,7},{... | collective-permute-start | bytes 49160 | tf_op jit(solution)/shard_map/ppermute | solution.py:18
  172.0 4.5 %all-reduce.13 = bf16[64,512]{1,0:T(8,128)(2,1)S(1)} all-reduce(f32[64,512]{1,0:T(8,128)} %get-tuple-element.30), channel_id=1, replica_groups=mesh['group'=2,'lat'=4,'lon'=2,'sub'=2] {'sub'}, use_global_device_ids=true, to_apply=%region_22.23 | all-reduce | flops 32768 | bytes 196608 | tf_op jit(solution)/shard_map/psum | solution.py:165
  180.5 6.2 %collective-permute-start.15 = (bf16[16,512]{1,0:T(8,128)(2,1)S(1)}, bf16[16,512]{1,0:T(8,128)(2,1)S(1)}, u32[]{:S(2)}, u32[]{:S(2)}) collective-permute-start(bf16[16,512]{1,0:T(8,128)(2,1)S(1)} %get-tuple-element.14), channel_id=1, source_target_pairs={{0,4},{4,8},{8,12},{1,5},{5,9},{9,13},{2,6},{6,10},{10,14},{3,7},{... | collective-permute-start | bytes 49160 | tf_op jit(solution)/shard_map/ppermute | solution.py:18
  186.7 3.9 %collective-permute-start.14 = (bf16[16,512]{1,0:T(8,128)(2,1)S(1)}, bf16[16,512]{1,0:T(8,128)(2,1)S(1)}, u32[]{:S(2)}, u32[]{:S(2)}) collective-permute-start(bf16[16,512]{1,0:T(8,128)(2,1)S(1)} %get-tuple-element.15), channel_id=1, source_target_pairs={{0,4},{4,8},{8,12},{1,5},{5,9},{9,13},{2,6},{6,10},{10,14},{3,7},{... | collective-permute-start | bytes 49160 | tf_op jit(solution)/shard_map/ppermute | solution.py:18
  203.2 4.9 %gather_fusion.3 = f32[1024,512]{1,0:T(8,128)} fusion(f32[64,512]{1,0:T(8,128)S(1)} %subtract_multiply_fusion.2, s32[1024]{0:T(1024)S(1)} %get-tuple-element.36), kind=kCustom, calls=%fused_computation.3 | custom fusion | bytes 4198400 | tf_op jit(solution)/shard_map/gather | solution.py:176
  209.9 3.5 %reshape.247 = f32[512,2,512]{2,1,0:T(2,128)} reshape(f32[1024,512]{1,0:T(8,128)} %gather_fusion.3) | data formatting | bytes 4194304 | tf_op jit(solution)/shard_map/gather | solution.py:176
  216.0 4.9 %fusion.55 = (bf16[512,512]{1,0:T(8,128)(2,1)S(1)}, bf16[512,2,512]{2,0,1:T(8,128)(2,1)}) fusion(f32[512]{0:T(512)S(1)} %copy-done.25, f32[512,2,512]{2,1,0:T(2,128)} %reshape.302, f32[512,512]{1,0:T(8,128)} %copy-done.8, bf16[512,512]{1,0:T(8,128)(2,1)S(1)} %copy-done, f32[512,2,512]{2,1,0:T(2,128)} %reshape.247, ...), kind=kOutput, calls=%fused_computation.148 | convolution fusion | flops 547094528 | bytes 9459712 | tf_op jit(solution)/shard_map/ske,de->skd/dot_general | solution.py:177
  222.2 5.2 %all-to-all-start.2 = ((bf16[4,128,512]{2,1,0:T(8,128)(2,1)}), bf16[4,128,512]{2,1,0:T(8,128)(2,1)S(1)}, u32[]{:S(2)}, u32[]{:S(2)}) async-start(bf16[4,128,512]{2,1,0:T(8,128)(2,1)} %bitcast.31), calls=%async_computation.2 | async-start | bytes 1048576 | tf_op jit(solution)/shard_map/all_to_all | solution.py:184
  232.0 18.3 %all-reduce.12.cloned.1.call-done = bf16[64,512]{1,0:T(8,128)(2,1)} async-done(((bf16[64,512]{1,0:T(8,128)(2,1)}), bf16[64,512]{1,0:T(8,128)(2,1)}) %all-reduce.12.cloned.1.call-update) | async-done | bytes 65552 | tf_op jit(solution)/shard_map/psum | solution.py:180
  (210 shorter events, 88.1 us)
Async XLA Ops:
  13.7 11.9 %all-to-all-start = ((s32[4,128,2]{1,2,0:T(2,128)}), s32[4,128,2]{1,2,0:T(2,128)S(1)}, u32[]{:S(2)}, u32[]{:S(2)}) async-start(s32[4,128,2]{1,2,0:T(2,128)} %copy.39), calls=%async_computation | async-start | bytes 8192 | tf_op jit(solution)/shard_map/all_to_all | solution.py:122
  25.6 17.5 %all-to-all-start.1 = ((bf16[4,128,512]{2,1,0:T(8,128)(2,1)}), bf16[4,128,512]{2,1,0:T(8,128)(2,1)S(1)}, u32[]{:S(2)}, u32[]{:S(2)}) async-start(bf16[4,128,512]{2,1,0:T(8,128)(2,1)} %bitcast.7), calls=%async_computation.1 | async-start | bytes 1048576 | tf_op jit(solution)/shard_map/all_to_all | solution.py:121
  29.1 44.5 %all-reduce.6.cloned.1.call-start = ((), (), s32[]{:S(2)}) async-start(), calls=%async_computation.3 | async-start | bytes 262144 | tf_op jit(solution)/shard_map/psum | solution.py:137
  56.4 75.8 %all-reduce.8.cloned.1.call-start = ((), (), s32[]{:S(2)}) async-start(), calls=%async_computation.4 | async-start | bytes 262144 | tf_op jit(solution)/shard_map/psum | solution.py:154
  77.9 7.8 %collective-permute-start = (bf16[16,512]{1,0:T(8,128)(2,1)S(1)}, bf16[16,512]{1,0:T(8,128)(2,1)S(1)}, u32[]{:S(2)}, u32[]{:S(2)}) collective-permute-start(bf16[16,512]{1,0:T(8,128)(2,1)S(1)} %get-tuple-element.25), channel_id=1, source_target_pairs={{0,2},{2,0},{1,3},{3,1},{4,6},{6,4},{5,7},{7,5},{8,10},{10,8},{9,1... | collective-permute-start | bytes 49160 | tf_op jit(solution)/shard_map/ppermute | solution.py:12
  79.7 18.6 %collective-permute-start.10 = (bf16[16,512]{1,0:T(8,128)(2,1)S(1)}, bf16[16,512]{1,0:T(8,128)(2,1)S(1)}, u32[]{:S(2)}, u32[]{:S(2)}) collective-permute-start(bf16[16,512]{1,0:T(8,128)(2,1)S(1)} %get-tuple-element.18), channel_id=1, source_target_pairs={{0,2},{2,0},{1,3},{3,1},{4,6},{6,4},{5,7},{7,5},{8,10},{10,8},{9,1... | collective-permute-start | bytes 49160 | tf_op jit(solution)/shard_map/ppermute | solution.py:12
  80.0 29.2 %collective-permute-start.9 = (bf16[16,512]{1,0:T(8,128)(2,1)S(1)}, bf16[16,512]{1,0:T(8,128)(2,1)S(1)}, u32[]{:S(2)}, u32[]{:S(2)}) collective-permute-start(bf16[16,512]{1,0:T(8,128)(2,1)S(1)} %get-tuple-element.19), channel_id=1, source_target_pairs={{0,4},{4,8},{8,12},{1,5},{5,9},{9,13},{2,6},{6,10},{10,14},{3,7},{... | collective-permute-start | bytes 49160 | tf_op jit(solution)/shard_map/ppermute | solution.py:18
  83.6 16.2 %collective-permute-start.7 = (bf16[16,512]{1,0:T(8,128)(2,1)S(1)}, bf16[16,512]{1,0:T(8,128)(2,1)S(1)}, u32[]{:S(2)}, u32[]{:S(2)}) collective-permute-start(bf16[16,512]{1,0:T(8,128)(2,1)S(1)} %get-tuple-element.20), channel_id=1, source_target_pairs={{0,2},{2,0},{1,3},{3,1},{4,6},{6,4},{5,7},{7,5},{8,10},{10,8},{9,1... | collective-permute-start | bytes 49160 | tf_op jit(solution)/shard_map/ppermute | solution.py:12
  85.1 7.5 %collective-permute-start.3 = (bf16[16,512]{1,0:T(8,128)(2,1)S(1)}, bf16[16,512]{1,0:T(8,128)(2,1)S(1)}, u32[]{:S(2)}, u32[]{:S(2)}) collective-permute-start(bf16[16,512]{1,0:T(8,128)(2,1)S(1)} %get-tuple-element.23), channel_id=1, source_target_pairs={{0,2},{2,0},{1,3},{3,1},{4,6},{6,4},{5,7},{7,5},{8,10},{10,8},{9,1... | collective-permute-start | bytes 49160 | tf_op jit(solution)/shard_map/ppermute | solution.py:12
  85.7 5.6 %collective-permute-start.1 = (bf16[16,512]{1,0:T(8,128)(2,1)S(1)}, bf16[16,512]{1,0:T(8,128)(2,1)S(1)}, u32[]{:S(2)}, u32[]{:S(2)}) collective-permute-start(bf16[16,512]{1,0:T(8,128)(2,1)S(1)} %collective-permute-done), channel_id=1, source_target_pairs={{4,0},{8,4},{12,8},{5,1},{9,5},{13,9},{6,2},{10,6},{14,10},{7,3},{... | collective-permute-start | bytes 49160 | tf_op jit(solution)/shard_map/ppermute | solution.py:18
  91.3 5.6 %collective-permute-start.2 = (bf16[16,512]{1,0:T(8,128)(2,1)S(1)}, bf16[16,512]{1,0:T(8,128)(2,1)S(1)}, u32[]{:S(2)}, u32[]{:S(2)}) collective-permute-start(bf16[16,512]{1,0:T(8,128)(2,1)S(1)} %get-tuple-element.24), channel_id=1, source_target_pairs={{4,0},{8,4},{12,8},{5,1},{9,5},{13,9},{6,2},{10,6},{14,10},{7,3},{... | collective-permute-start | bytes 49160 | tf_op jit(solution)/shard_map/ppermute | solution.py:18
  92.6 15.3 %collective-permute-start.6 = (bf16[16,512]{1,0:T(8,128)(2,1)S(1)}, bf16[16,512]{1,0:T(8,128)(2,1)S(1)}, u32[]{:S(2)}, u32[]{:S(2)}) collective-permute-start(bf16[16,512]{1,0:T(8,128)(2,1)S(1)} %get-tuple-element.21), channel_id=1, source_target_pairs={{0,2},{2,0},{1,3},{3,1},{4,6},{6,4},{5,7},{7,5},{8,10},{10,8},{9,1... | collective-permute-start | bytes 49160 | tf_op jit(solution)/shard_map/ppermute | solution.py:12
  96.9 7.4 %collective-permute-start.4 = (bf16[16,512]{1,0:T(8,128)(2,1)S(1)}, bf16[16,512]{1,0:T(8,128)(2,1)S(1)}, u32[]{:S(2)}, u32[]{:S(2)}) collective-permute-start(bf16[16,512]{1,0:T(8,128)(2,1)S(1)} %collective-permute-done.3), channel_id=1, source_target_pairs={{4,0},{8,4},{12,8},{5,1},{9,5},{13,9},{6,2},{10,6},{14,10},{7,3},{... | collective-permute-start | bytes 49160 | tf_op jit(solution)/shard_map/ppermute | solution.py:18
  98.3 9.7 %collective-permute-start.5 = (bf16[16,512]{1,0:T(8,128)(2,1)S(1)}, bf16[16,512]{1,0:T(8,128)(2,1)S(1)}, u32[]{:S(2)}, u32[]{:S(2)}) collective-permute-start(bf16[16,512]{1,0:T(8,128)(2,1)S(1)} %get-tuple-element.22), channel_id=1, source_target_pairs={{0,2},{2,0},{1,3},{3,1},{4,6},{6,4},{5,7},{7,5},{8,10},{10,8},{9,1... | collective-permute-start | bytes 49160 | tf_op jit(solution)/shard_map/ppermute | solution.py:12
  99.8 9.4 %collective-permute-start.11 = (bf16[16,512]{1,0:T(8,128)(2,1)S(1)}, bf16[16,512]{1,0:T(8,128)(2,1)S(1)}, u32[]{:S(2)}, u32[]{:S(2)}) collective-permute-start(bf16[16,512]{1,0:T(8,128)(2,1)S(1)} %collective-permute-done.10), channel_id=1, source_target_pairs={{0,4},{4,8},{8,12},{1,5},{5,9},{9,13},{2,6},{6,10},{10,14},{3,7},{... | collective-permute-start | bytes 49160 | tf_op jit(solution)/shard_map/ppermute | solution.py:18
  114.2 50.2 %all-reduce.10.cloned.1.call-start = ((), (), s32[]{:S(2)}) async-start(), calls=%async_computation.5 | async-start | bytes 786432 | tf_op jit(solution)/shard_map/psum | solution.py:165
  170.6 16.1 %collective-permute-start.13 = (bf16[16,512]{1,0:T(8,128)(2,1)}, bf16[16,512]{1,0:T(8,128)(2,1)}, u32[]{:S(2)}, u32[]{:S(2)}) collective-permute-start(bf16[16,512]{1,0:T(8,128)(2,1)} %collective-permute-done.12), channel_id=1, source_target_pairs={{0,2},{2,0},{1,3},{3,1},{4,6},{6,4},{5,7},{7,5},{8,10},{10,8},{9,1... | collective-permute-start | bytes 49160 | tf_op jit(solution)/shard_map/ppermute | solution.py:12
  176.6 16.8 %collective-permute-start.22 = (bf16[16,512]{1,0:T(8,128)(2,1)S(1)}, bf16[16,512]{1,0:T(8,128)(2,1)S(1)}, u32[]{:S(2)}, u32[]{:S(2)}) collective-permute-start(bf16[16,512]{1,0:T(8,128)(2,1)S(1)} %get-tuple-element.9), channel_id=1, source_target_pairs={{4,0},{8,4},{12,8},{5,1},{9,5},{13,9},{6,2},{10,6},{14,10},{7,3},{... | collective-permute-start | bytes 49160 | tf_op jit(solution)/shard_map/ppermute | solution.py:18
  177.9 21.6 %collective-permute-start.21 = (bf16[16,512]{1,0:T(8,128)(2,1)S(1)}, bf16[16,512]{1,0:T(8,128)(2,1)S(1)}, u32[]{:S(2)}, u32[]{:S(2)}) collective-permute-start(bf16[16,512]{1,0:T(8,128)(2,1)S(1)} %get-tuple-element.10), channel_id=1, source_target_pairs={{4,0},{8,4},{12,8},{5,1},{9,5},{13,9},{6,2},{10,6},{14,10},{7,3},{... | collective-permute-start | bytes 49160 | tf_op jit(solution)/shard_map/ppermute | solution.py:18
  179.2 14.9 %collective-permute-start.19 = (bf16[16,512]{1,0:T(8,128)(2,1)S(1)}, bf16[16,512]{1,0:T(8,128)(2,1)S(1)}, u32[]{:S(2)}, u32[]{:S(2)}) collective-permute-start(bf16[16,512]{1,0:T(8,128)(2,1)S(1)} %get-tuple-element.11), channel_id=1, source_target_pairs={{4,0},{8,4},{12,8},{5,1},{9,5},{13,9},{6,2},{10,6},{14,10},{7,3},{... | collective-permute-start | bytes 49160 | tf_op jit(solution)/shard_map/ppermute | solution.py:18
  180.5 10.9 %collective-permute-start.15 = (bf16[16,512]{1,0:T(8,128)(2,1)S(1)}, bf16[16,512]{1,0:T(8,128)(2,1)S(1)}, u32[]{:S(2)}, u32[]{:S(2)}) collective-permute-start(bf16[16,512]{1,0:T(8,128)(2,1)S(1)} %get-tuple-element.14), channel_id=1, source_target_pairs={{0,4},{4,8},{8,12},{1,5},{5,9},{9,13},{2,6},{6,10},{10,14},{3,7},{... | collective-permute-start | bytes 49160 | tf_op jit(solution)/shard_map/ppermute | solution.py:18
  191.3 5.8 %collective-permute-start.18 = (bf16[16,512]{1,0:T(8,128)(2,1)S(1)}, bf16[16,512]{1,0:T(8,128)(2,1)S(1)}, u32[]{:S(2)}, u32[]{:S(2)}) collective-permute-start(bf16[16,512]{1,0:T(8,128)(2,1)S(1)} %get-tuple-element.12), channel_id=1, source_target_pairs={{0,2},{2,0},{1,3},{3,1},{4,6},{6,4},{5,7},{7,5},{8,10},{10,8},{9,1... | collective-permute-start | bytes 49160 | tf_op jit(solution)/shard_map/ppermute | solution.py:12
  222.2 29.8 %all-to-all-start.2 = ((bf16[4,128,512]{2,1,0:T(8,128)(2,1)}), bf16[4,128,512]{2,1,0:T(8,128)(2,1)S(1)}, u32[]{:S(2)}, u32[]{:S(2)}) async-start(bf16[4,128,512]{2,1,0:T(8,128)(2,1)} %bitcast.31), calls=%async_computation.2 | async-start | bytes 1048576 | tf_op jit(solution)/shard_map/all_to_all | solution.py:184
  227.4 22.9 %all-reduce.12.cloned.1.call-start = ((), (), s32[]{:S(2)}) async-start(), calls=%async_computation.6 | async-start | bytes 131072 | tf_op jit(solution)/shard_map/psum | solution.py:180
  (33 other events, 579.2 us)
Sparse Core Ops, SparseCore 0:
  56.5 17.0 all-reduce.5
  114.3 17.8 all-reduce.7
  144.7 19.6 all-reduce.9
  232.1 18.1 all-reduce.11
where the time goes:
time: 262 us; the launch traced here: 260 us
  waiting for transfers between devices  90.7 us (35%)
  starting transfers between devices  62.9 us (24%)
  local copies, waits for them, and re-layouts  42.3 us (16%)
  matrix products  25.7 us (10%)
  other arithmetic  19.7 us (8%)
  between operations  14.6 us (6%)
  blocking collectives  4.52 us (2%)
    ppermute x12, starting transfers between devices, passed_along_2(): return lax.ppermute(block, axis, route)  33.8 us
    psum x1, waiting for transfers between devices, on_device(): d_table, d_recv = lax.psum((d_table_local, d_recv_local), 'sub')  19.8 us
    psum x1, waiting for transfers between devices, on_device(): d_proj_mesh = lax.psum(d_proj_local.astype(jnp.bfloat16), 'sub')  18.3 us
    psum x1, waiting for transfers between devices, on_device(): agg_mesh = lax.psum(jnp.sum(layer_norm(z_mesh), 1), 'sub')  17.7 us
    psum x1, waiting for transfers between devices, on_device(): agg_grid = lax.psum(agg_local, 'sub')  17 us
    ppermute x12, starting transfers between devices, passed_along(): lax.ppermute(shard, axis, [(i, (i + by) % devices) for i in range(devices)])  14 us
    gather x2, local copies, waits for them, and re-layouts, on_device(): d_agg_grid[safe_rows]  8.36 us
    ppermute x12, waiting for transfers between devices, passed_along_2(): return lax.ppermute(block, axis, route)  6.79 us
  transfers between devices with their start and end apart: 31, of which 13 were waited for; matrix products, arithmetic and copies ran while one was open for 8% of the time, Pallas kernels for 0%

commit v1 on v0

v1 whole, which is shorter than its diff:
```python
import functools

import jax
import jax.numpy as jnp
from jax import lax
from jax.experimental import pallas as pl
from jax.experimental.pallas import tpu as pltpu
from jax.sharding import PartitionSpec as P

EPS = 1e-05
DIRECTIONS = ((-1, -1), (-1, 0), (-1, 1), (0, -1), (0, 1), (1, -1), (1, 0), (1, 1))
MESH = pl.DeviceIdType.MESH
F32 = jnp.float32
BF16 = jnp.bfloat16
CHUNK = 64


def dot_plain(left, right):
    return jnp.dot(left, right, preferred_element_type=F32)


def dot_trans(left, right):
    return lax.dot_general(left, right, (((1,), (1,)), ((), ())), preferred_element_type=F32)


def row_mean(value):
    return jnp.mean(value, -1, keepdims=True)


def norm_parts(value):
    centred = value - row_mean(value)
    inverse = lax.rsqrt(row_mean(centred * centred) + EPS)
    return centred * inverse, inverse


def norm_back(normed, inverse, upstream):
    inner = row_mean(upstream * normed)
    return (upstream - row_mean(upstream) - normed * inner) * inverse


def silu_slope(value):
    sigma = jax.nn.sigmoid(value)
    return sigma * (1.0 + value * (1.0 - sigma))


def iota_f32(shape, axis):
    return lax.broadcasted_iota(jnp.int32, shape, axis).astype(F32)


def as_row(column):
    n = column.shape[0]
    shape = (n, n)
    same = lax.broadcasted_iota(jnp.int32, shape, 0) == lax.broadcasted_iota(jnp.int32, shape, 1)
    return jnp.sum(jnp.where(same, column, 0.0), 0, keepdims=True)


def hot_rows(column, count):
    return (column == iota_f32((column.shape[0], count), 1)).astype(F32).astype(BF16)


def hot_columns(row, count):
    return (row == iota_f32((count, row.shape[1]), 0)).astype(F32).astype(BF16)


def kernel(
    bands,
    sectors,
    grid_ref,
    band_ref,
    rows_ref,
    mesh_ref,
    slots_ref,
    send_ref,
    enc_send_hbm,
    enc_recv_hbm,
    enc_edge_hbm,
    bias_grid_ref,
    node_gain_ref,
    proc_send_hbm,
    proc_recv_hbm,
    proc_edge_hbm,
    bias_mesh_ref,
    mesh_gain_ref,
    cot_ref,
    mesh_out_ref,
    mesh_grad_ref,
    grid_grad_ref,
    enc_send,
    enc_recv,
    enc_edge,
    proc_send,
    proc_recv,
    proc_edge,
    slots_mine,
    slots_peer,
    gathered_mesh,
    proj_grid,
    pre_grid,
    z_grid,
    inv_grid,
    hid,
    work,
    part_mine,
    part_out,
    part_in,
    lat_out,
    lat_in,
    mid_full,
    bound_out,
    table,
    pre_mesh,
    z_mesh,
    out_half_peer,
    out_half_mine,
    back_out,
    back_in,
    send_part_out,
    send_part_in,
    d_agg_all,
    part_out_2,
    part_in_2,
    lat_out_2,
    lat_in_2,
    grad_half_mine,
    grad_half_peer,
    w_sem,
    lat_s,
    lat_r,
    fwd_s,
    fwd_r,
    sub_s,
    sub_r,
    nb_s,
    nb_r,
):
    lat, lon, sub = lax.axis_index("lat"), lax.axis_index("lon"), lax.axis_index("sub")
    other = 1 - sub
    nodes, width = grid_ref.shape
    fanout = rows_ref.shape[1]
    mesh_rows = mesh_ref.shape[0]
    half = mesh_rows // 2
    half_all = bands * half
    bound = send_ref.shape[2]
    edges_half = 2 * slots_ref.shape[1]
    table_rows = table.shape[0]

    weights = (
        (enc_send_hbm, enc_send),
        (enc_recv_hbm, enc_recv),
        (enc_edge_hbm, enc_edge),
        (proc_send_hbm, proc_send),
        (proc_recv_hbm, proc_recv),
        (proc_edge_hbm, proc_edge),
    )
    loads = [pltpu.make_async_copy(a, b, w_sem.at[n]) for n, (a, b) in enumerate(weights)]
    for load in loads:
        load.start()

    slots_mine[...] = jnp.zeros_like(slots_mine)
    slots_mine[:, 0 : slots_ref.shape[1]] = slots_ref[...]
    table[mesh_rows:, :] = jnp.zeros((table_rows - mesh_rows, width), BF16)
    back_in[...] = jnp.zeros_like(back_in)

    barrier = pltpu.get_barrier_semaphore()

    def lat_peer(step):
        return lax.rem(lat + step, bands)

    def reaches(d):
        target = lat + DIRECTIONS[d][0]
        return (target >= 0) & (target < bands)

    def comes_from(d):
        target = lat - DIRECTIONS[d][0]
        return (target >= 0) & (target < bands)

    def neighbour(d, sign):
        return {
            "lat": lat + sign * DIRECTIONS[d][0],
            "lon": lax.rem(lon + sign * DIRECTIONS[d][1] + sectors, sectors),
        }

    for step in range(1, bands):
        pl.semaphore_signal(barrier, inc=1, device_id={"lat": lat_peer(step)}, device_id_type=MESH)
    pl.semaphore_signal(barrier, inc=1, device_id={"sub": other}, device_id_type=MESH)
    diagonal = [d for d in range(8) if DIRECTIONS[d][1] != 0]
    for d in diagonal:
        @pl.when(reaches(d))
        def _():
            pl.semaphore_signal(barrier, inc=1, device_id=neighbour(d, 1), device_id_type=MESH)
    near = 2 + 2 * (lat > 0).astype(jnp.int32) + 2 * (lat < bands - 1).astype(jnp.int32)
    pl.semaphore_wait(barrier, bands + near)

    def half_rows(which, band):
        return pl.ds(pl.multiple_of(which * half_all + band * half, half), half)

    def band_rows(band):
        return pl.ds(pl.multiple_of(band * half, half), half)

    my_rows = pl.ds(pl.multiple_of(sub * half, half), half)
    peer_rows = pl.ds(pl.multiple_of(other * half, half), half)

    def to_sub(source, target, n):
        return pltpu.make_async_remote_copy(
            src_ref=source,
            dst_ref=target,
            send_sem=sub_s.at[n],
            recv_sem=sub_r.at[n],
            device_id={"sub": other},
            device_id_type=MESH,
        )

    def to_lat(source, target, n, step):
        return pltpu.make_async_remote_copy(
            src_ref=source,
            dst_ref=target,
            send_sem=lat_s.at[n, step],
            recv_sem=lat_r.at[n, step],
            device_id={"lat": lat_peer(step)},
            device_id_type=MESH,
        )

    def gather_start(source, whole, n):
        copies = []
        for step in range(1, bands):
            copy = to_lat(source, whole.at[half_rows(sub, lat)], n, step)
            copy.start()
            copies.append(copy)
        return copies

    def gather_finish(copies, whole, n):
        onward = []
        for step in range(1, bands):
            copies[step - 1].wait_recv()
            origin = lax.rem(lat - step + bands, bands)
            copy = pltpu.make_async_remote_copy(
                src_ref=whole.at[half_rows(sub, origin)],
                dst_ref=whole.at[half_rows(sub, origin)],
                send_sem=fwd_s.at[n, step],
                recv_sem=fwd_r.at[n, step],
                device_id={"sub": other},
                device_id_type=MESH,
            )
            copy.start()
            onward.append(copy)
        for copy in onward:
            copy.wait_recv()
        return onward

    slot_copy = to_sub(slots_mine.at[peer_rows], slots_peer, 0)
    slot_copy.start()
    gather_1 = gather_start(mesh_ref.at[my_rows], gathered_mesh, 0)
    gathered_mesh[half_rows(0, lat), :] = mesh_ref[0:half, :]
    gathered_mesh[half_rows(1, lat), :] = mesh_ref[half:, :]

    bias_grid = bias_grid_ref[...].reshape(1, width)
    bias_mesh = bias_mesh_ref[...].reshape(1, width)
    node_gain = node_gain_ref[...].reshape(1, width)
    mesh_gain = mesh_gain_ref[...].reshape(1, width)

    loads[0].wait()
    proj_grid[...] = dot_plain(grid_ref[...], enc_send[...]).astype(BF16)

    band_of = band_ref[...]
    hots, hots_t = [], []
    for k in range(fanout):
        row = rows_ref[:, k : k + 1]
        upper = (row >= half).astype(jnp.int32)
        place = (upper * (half_all - half) + band_of * half + row).astype(F32)
        hots.append(hot_rows(place, 2 * half_all))
        hots_t.append(hot_columns(as_row(place), 2 * half_all))
    hot_t = jnp.concatenate(hots_t, 1)

    listed = jnp.concatenate(
        [jnp.broadcast_to(send_ref[0, d : d + 1, :], (bound, bound)) for d in range(8)], 0
    ).astype(F32)
    lane = lax.broadcasted_iota(jnp.int32, (8 * bound, bound), 1)
    line = lax.rem(lax.broadcasted_iota(jnp.int32, (8 * bound, bound), 0), bound)
    list_column = jnp.sum(jnp.where(lane == line, listed, 0.0), 1, keepdims=True)
    pick = hot_rows(list_column, mesh_rows)
    pick_t = hot_columns(as_row(list_column), mesh_rows)

    slot_copy.wait()
    own_slots = slots_ref[my_rows, :].astype(F32)
    their_slots = slots_peer[...].astype(F32)
    slot_column = jnp.concatenate(
        [own_slots[:, k : k + 1] for k in range(edges_half // 2)]
        + [their_slots[:, k : k + 1] for k in range(edges_half // 2)],
        0,
    )
    slot_hot = hot_rows(slot_column, table_rows)
    slot_hot_t = hot_columns(as_row(slot_column), table_rows)

    loads[1].wait()
    loads[2].wait()
    onward_1 = gather_finish(gather_1, gathered_mesh, 0)
    proj_mesh = dot_plain(gathered_mesh[...], enc_recv[...]).astype(BF16)
    for k in range(fanout):
        base = k * nodes
        pre_grid[base : base + nodes, :] = dot_plain(hots[k], proj_mesh)
        for at in range(0, nodes, CHUNK):
            here = slice(base + at, base + at + CHUNK)
            pre = pre_grid[here, :] + proj_grid[at : at + CHUNK, :].astype(F32) + bias_grid
            pre_grid[here, :] = pre
            hid[here, :] = (pre * jax.nn.sigmoid(pre)).astype(BF16)
        z_grid[base : base + nodes, :] = dot_plain(hid[base : base + nodes, :], enc_edge[...])
        for at in range(base, base + nodes, CHUNK):
            here = slice(at, at + CHUNK)
            normed, inverse = norm_parts(z_grid[here, :])
            z_grid[here, :] = normed
            inv_grid[here, :] = inverse
            hid[here, :] = normed.astype(BF16)

    def scatter_sum(values, mine, out, inbound, out_lat, in_lat, n_sub, n_lat, meanwhile):
        total = dot_plain(hot_t, values)
        low, high = total[0:half_all, :], total[half_all:, :]
        out[...] = jnp.where(sub == 0, high, low).astype(BF16)
        copy = to_sub(out, inbound, n_sub)
        copy.start()
        mine[...] = jnp.where(sub == 0, low, high)
        meanwhile()
        copy.wait()
        copies = []
        for step in range(bands - 1, 0, -1):
            rows = band_rows(lat_peer(step))
            out_lat[rows, :] = (mine[rows, :] + inbound[rows, :].astype(F32)).astype(BF16)
            copy = to_lat(out_lat.at[rows], in_lat.at[step], n_lat, step)
            copy.start()
            copies.append(copy)
        rows = band_rows(lat)
        own = mine[rows, :] + inbound[rows, :].astype(F32)
        return own, copies

    def scatter_finish(own, copies, in_lat):
        for copy in copies:
            copy.wait()
        for step in range(1, bands):
            own = own + in_lat[step].astype(F32)
        return own

    def slope_of(ref, start, stop):
        for at in range(start, stop, CHUNK):
            ref[at : at + CHUNK, :] = silu_slope(ref[at : at + CHUNK, :])

    own, copies = scatter_sum(
        hid[...], part_mine, part_out, part_in, lat_out, lat_in, 1, 1, lambda: None
    )
    slope_of(pre_grid, 0, fanout * nodes)
    for n in range(3, 6):
        loads[n].wait()
    agg_grid = scatter_finish(own, copies, lat_in)

    agg_grid_normed, agg_grid_inverse = norm_parts(agg_grid)
    mid_half = (mesh_ref[my_rows, :].astype(F32) + agg_grid_normed * node_gain).astype(BF16)
    mid_full[my_rows, :] = mid_half
    mid_copy = to_sub(mid_full.at[my_rows], mid_full.at[my_rows], 2)
    mid_copy.start()
    recv_half = dot_plain(mid_half, proc_recv[...]).astype(BF16).astype(F32) + bias_mesh
    mid_copy.wait()
    send_mesh = dot_plain(mid_full[...], proc_send[...]).astype(BF16)
    bound_out[...] = dot_plain(pick, send_mesh).astype(BF16)

    def block_of(d):
        return pl.ds(d * bound, bound)

    def table_of(d):
        return pl.ds(mesh_rows + d * bound, bound)

    def to_near(source, target, n, d, sign):
        return pltpu.make_async_remote_copy(
            src_ref=source,
            dst_ref=target,
            send_sem=nb_s.at[n, d],
            recv_sem=nb_r.at[n, d],
            device_id=neighbour(d, sign),
            device_id_type=MESH,
        )

    for d in range(8):
        @pl.when(reaches(d))
        def _():
            to_near(bound_out.at[block_of(d)], table.at[table_of(d)], 0, d, 1).start()
    table[0:mesh_rows, :] = send_mesh
    for d in range(8):
        copy = to_near(bound_out.at[block_of(d)], table.at[table_of(d)], 0, d, 1)

        @pl.when(comes_from(d))
        def _():
            copy.wait_recv()

    edges = edges_half * half
    pre_mesh[...] = dot_plain(slot_hot, table[...])
    for at in range(0, edges, half):
        here = slice(at, at + half)
        pre = pre_mesh[here, :] + recv_half
        pre_mesh[here, :] = pre
        hid[here, :] = (pre * jax.nn.sigmoid(pre)).astype(BF16)
    z_mesh[...] = dot_plain(hid[0:edges, :], proc_edge[...])
    agg_mesh = jnp.zeros((half, width), F32)
    inverses = []
    for at in range(0, edges, half):
        here = slice(at, at + half)
        normed, inverse = norm_parts(z_mesh[here, :])
        z_mesh[here, :] = normed
        inverses.append(inverse)
        agg_mesh = agg_mesh + normed

    agg_mesh_normed, agg_mesh_inverse = norm_parts(agg_mesh)
    out_half = (mid_half.astype(F32) + agg_mesh_normed * mesh_gain).astype(BF16)
    out_half_mine[...] = out_half
    mesh_out_ref[my_rows, :] = out_half
    out_copy = to_sub(out_half_mine, out_half_peer, 3)
    out_copy.start()

    upstream = cot_ref[my_rows, :].astype(F32)
    d_agg_mesh = norm_back(agg_mesh_normed, agg_mesh_inverse, upstream * mesh_gain)
    for n, at in enumerate(range(0, edges, half)):
        here = slice(at, at + half)
        hid[here, :] = norm_back(z_mesh[here, :], inverses[n], d_agg_mesh).astype(BF16)
    work[0:edges, :] = dot_trans(hid[0:edges, :], proc_edge[...])
    d_recv = jnp.zeros((half, width), F32)
    for at in range(0, edges, half):
        here = slice(at, at + half)
        d_pre = (work[here, :] * silu_slope(pre_mesh[here, :])).astype(BF16)
        hid[here, :] = d_pre
        d_recv = d_recv + d_pre.astype(F32)
    d_table = dot_plain(slot_hot_t, hid[0:edges, :])
    back_out[...] = d_table[mesh_rows : mesh_rows + 8 * bound, :].astype(BF16)
    for d in range(8):
        @pl.when(comes_from(d))
        def _():
            to_near(back_out.at[block_of(d)], back_in.at[block_of(d)], 1, d, -1).start()
    d_mid = upstream + dot_trans(d_recv.astype(BF16), proc_recv[...])
    for d in range(8):
        copy = to_near(back_out.at[block_of(d)], back_in.at[block_of(d)], 1, d, -1)

        @pl.when(reaches(d))
        def _():
            copy.wait_recv()
    d_send = d_table[0:mesh_rows, :] + dot_plain(pick_t, back_in[...])
    send_part_out[...] = jnp.where(sub == 0, d_send[half:, :], d_send[0:half, :])
    send_copy = to_sub(send_part_out, send_part_in, 4)
    send_copy.start()
    d_send_half = jnp.where(sub == 0, d_send[0:half, :], d_send[half:, :])
    send_copy.wait()
    d_send_half = d_send_half + send_part_in[...]
    d_mid = d_mid + dot_trans(d_send_half.astype(BF16), proc_send[...])
    d_agg_grid = norm_back(agg_grid_normed, agg_grid_inverse, d_mid * node_gain)
    d_agg_all[half_rows(sub, lat), :] = d_agg_grid.astype(BF16)
    own_copy = to_sub(d_agg_all.at[half_rows(sub, lat)], d_agg_all.at[half_rows(sub, lat)], 5)
    own_copy.start()
    gather_2 = gather_start(d_agg_all.at[half_rows(sub, lat)], d_agg_all, 2)
    out_copy.wait()
    mesh_out_ref[peer_rows, :] = out_half_peer[...]
    onward_2 = gather_finish(gather_2, d_agg_all, 1)
    own_copy.wait()

    for k in range(fanout):
        base = k * nodes
        work[base : base + nodes, :] = dot_plain(hots[k], d_agg_all[...])
        for at in range(base, base + nodes, CHUNK):
            here = slice(at, at + CHUNK)
            hid[here, :] = norm_back(z_grid[here, :], inv_grid[here, :], work[here, :]).astype(BF16)
        work[base : base + nodes, :] = dot_trans(hid[base : base + nodes, :], enc_edge[...])
        for at in range(base, base + nodes, CHUNK):
            here = slice(at, at + CHUNK)
            hid[here, :] = (work[here, :] * pre_grid[here, :]).astype(BF16)

    def grid_side():
        total = hid[0:nodes, :].astype(F32)
        for k in range(1, fanout):
            total = total + hid[k * nodes : (k + 1) * nodes, :].astype(F32)
        grid_grad_ref[...] = dot_trans(total.astype(BF16), enc_send[...]).astype(BF16)

    own, copies_2 = scatter_sum(
        hid[...], part_mine, part_out_2, part_in_2, lat_out_2, lat_in_2, 6, 3, lambda: None
    )
    grid_side()
    d_proj_mesh = scatter_finish(own, copies_2, lat_in_2)
    grad_half = (d_mid + dot_trans(d_proj_mesh.astype(BF16), enc_recv[...])).astype(BF16)
    grad_half_mine[...] = grad_half
    grad_copy = to_sub(grad_half_mine, grad_half_peer, 7)
    grad_copy.start()
    mesh_grad_ref[my_rows, :] = grad_half
    for copy in gather_1 + gather_2 + onward_1 + onward_2:
        copy.wait_send()
    for d in range(8):
        @pl.when(reaches(d))
        def _():
            to_near(bound_out.at[block_of(d)], table.at[table_of(d)], 0, d, 1).wait_send()

        @pl.when(comes_from(d))
        def _():
            to_near(back_out.at[block_of(d)], back_in.at[block_of(d)], 1, d, -1).wait_send()
    grad_copy.wait()
    mesh_grad_ref[peer_rows, :] = grad_half_peer[...]


def on_device(bands, sectors, *args):
    grid_latent, mesh_latent, mesh_slots = args[0], args[3], args[4]
    send_rows, edge_rows = args[5], args[2]
    nodes, width = grid_latent.shape
    mesh_rows = mesh_latent.shape[0]
    half = mesh_rows // 2
    bound = 8 * send_rows.shape[2]
    table_rows = -(-(mesh_rows + bound) // 128) * 128
    edges = edge_rows.shape[1] * nodes
    mesh_edges = 2 * mesh_slots.shape[1] * half
    every = bands * mesh_rows
    most = max(edges, mesh_edges)
    vmem = pl.BlockSpec(memory_space=pltpu.VMEM)
    hbm = pl.BlockSpec(memory_space=pl.ANY)
    weights = (6, 7, 8, 11, 12, 13)
    dma = pltpu.SemaphoreType.DMA
    return pl.pallas_call(
        functools.partial(kernel, bands, sectors),
        out_shape=(
            jax.ShapeDtypeStruct((mesh_rows, width), BF16),
            jax.ShapeDtypeStruct((mesh_rows, width), BF16),
            jax.ShapeDtypeStruct((nodes, width), BF16),
        ),
        in_specs=[hbm if n in weights else vmem for n in range(len(args))],
        out_specs=(vmem, vmem, vmem),
        scratch_shapes=[pltpu.VMEM((width, width), BF16)] * 6
        + [
            pltpu.VMEM((mesh_rows, 128), jnp.int32),
            pltpu.VMEM((half, 128), jnp.int32),
            pltpu.VMEM((every, width), BF16),
            pltpu.VMEM((nodes, width), BF16),
            pltpu.VMEM((edges, width), F32),
            pltpu.VMEM((edges, width), F32),
            pltpu.VMEM((edges, 1), F32),
            pltpu.VMEM((most, width), BF16),
            pltpu.VMEM((most, width), F32),
            pltpu.VMEM((every // 2, width), F32),
            pltpu.VMEM((every // 2, width), BF16),
            pltpu.VMEM((every // 2, width), BF16),
            pltpu.VMEM((every // 2, width), BF16),
            pltpu.VMEM((bands, half, width), BF16),
            pltpu.VMEM((mesh_rows, width), BF16),
            pltpu.VMEM((bound, width), BF16),
            pltpu.VMEM((table_rows, width), BF16),
            pltpu.VMEM((mesh_edges, width), F32),
            pltpu.VMEM((mesh_edges, width), F32),
            pltpu.VMEM((half, width), BF16),
            pltpu.VMEM((half, width), BF16),
            pltpu.VMEM((bound, width), BF16),
            pltpu.VMEM((bound, width), BF16),
            pltpu.VMEM((half, width), F32),
            pltpu.VMEM((half, width), F32),
            pltpu.VMEM((every, width), BF16),
            pltpu.VMEM((every // 2, width), BF16),
            pltpu.VMEM((every // 2, width), BF16),
            pltpu.VMEM((every // 2, width), BF16),
            pltpu.VMEM((bands, half, width), BF16),
            pltpu.VMEM((half, width), BF16),
            pltpu.VMEM((half, width), BF16),
            dma((6,)),
            dma((4, bands)),
            dma((4, bands)),
            dma((2, bands)),
            dma((2, bands)),
            dma((8,)),
            dma((8,)),
            dma((2, 8)),
            dma((2, 8)),
        ],
        compiler_params=pltpu.CompilerParams(
            collective_id=0, has_side_effects=True, vmem_limit_bytes=48 * 1024 * 1024
        ),
    )(*args)


def solution(mesh):
    part = P(("group", "lat", "lon"), None)
    node = P(("group", "lat", "lon", "sub"), None)
    placed = (
        (node, node, node, part, P(("group", "lat", "lon"), "sub"))
        + (P(("group", "lat", "lon"), None, None),)
        + (P(),) * 10
        + (part,)
    )
    return jax.shard_map(
        functools.partial(on_device, mesh.shape["lat"], mesh.shape["lon"]),
        mesh=mesh,
        in_specs=placed,
        out_specs=(part, part, node),
        check_vma=False,
    )
```

time: 262 us -> 59.2 us (0.23)
  waiting for transfers between devices: 90.7 us -> 0 us
  starting transfers between devices: 62.9 us -> 0 us
  Pallas kernels: 0 us -> 46.2 us
  local copies, waits for them, and re-layouts: 42.3 us -> 11.7 us
  matrix products: 25.7 us -> 0 us
  other arithmetic: 19.7 us -> 0 us
  between operations: 14.6 us -> 0.77 us
  blocking collectives: 4.52 us -> 0 us
    psum x4 -> x0, waiting for transfers between devices: 72.9 us -> none  [the longest x1 19.8 us: on_device(): d_table, d_recv = lax.psum((d_table_local, d_recv_local), 'sub')]
    ppermute x24 -> x0, starting transfers between devices: 47.8 us -> none  [the longest x12 33.8 us: passed_along_2(): return lax.ppermute(block, axis, route)]
    pallas_call x0 -> x1, Pallas kernels: none -> 46.2 us  [on_device(): pl.pallas_call(functools.partial(kernel, bands, sectors), out_shape=(jax....]
    dot_general x16 -> x0, matrix products: 25.7 us -> none  [the longest x1 4.92 us: on_device(): jnp.einsum('ske,de->skd', d_z_grid, enc_edge, preferred_element_type=jnp....]
    gather x6 -> x0, local copies, waits for them, and re-layouts: 16.2 us -> none  [the longest x2 8.36 us: on_device(): d_agg_grid[safe_rows]]
    all_to_all x3 -> x0, starting transfers between devices: 15 us -> none  [the longest x1 6.32 us: on_device(): lax.all_to_all(target_out, 'lat', split_axis=0, concat_axis=0, tiled=True)]
    reduce_sum x13 -> x0, other arithmetic: 13.5 us -> none  [the longest x3 4.66 us: norm_back(): jnp.mean(upstream, -1, keepdims=True)]
    ppermute x24 -> x0, waiting for transfers between devices: 9.57 us -> none  [the longest x12 6.79 us: passed_along_2(): return lax.ppermute(block, axis, route)]
  transfers between devices with their start and end apart: 31 -> 0, of which waited for: 13 -> 0; matrix products, arithmetic and copies ran while one was open for 8% -> 0% of each run, Pallas kernels for 0% -> 0%
where the time goes in v1:
time: 59.2 us; the launch traced here: 58.7 us
  Pallas kernels  46.2 us (78%)
  local copies, waits for them, and re-layouts  11.7 us (20%)
  between operations  0.77 us (1%)
    pallas_call x1, Pallas kernels, on_device(): pl.pallas_call(functools.partial(kernel, bands, sectors), out_shape=(jax....  46.2 us
    unnamed x36, local copies, waits for them, and re-layouts  11.7 us

profile of v1, /device:TPU:0, one launch (start us, length us, event | category | flops | bytes accessed | tf_op | source)
XLA Modules:
  0.0 58.7 jit_solution(16148172667852616709)
XLA Ops:
  0.7 0.8 %copy.22.slots_ref = s32[64,4]{1,0:T(8,128)S(1)} copy(s32[64,4]{0,1:T(4,128)} %param.21) | data formatting | bytes 2048 | tf_op args[4]
  1.5 0.1 copy.20.band_ref
  1.6 0.0 copy-start.9
  1.6 0.0 copy-start.10
  1.6 0.0 copy-start.11
  1.6 0.0 copy-start.12
  1.7 0.0 copy-start.13
  1.7 0.8 %copy.21.rows_ref = s32[256,2]{1,0:T(8,128)S(1)} copy(s32[256,2]{0,1:T(2,128)} %param.19) | data formatting | bytes 4096 | tf_op args[2]
  2.5 0.0 copy-done.6
  2.5 0.0 copy-done.9
  2.5 0.0 copy-done.10
  2.6 0.0 copy-start
  2.6 1.0 %copy-done = bf16[512,512]{1,0:T(8,128)(2,1)S(1)} copy-done((bf16[512,512]{1,0:T(8,128)(2,1)S(1)}, bf16[512,512]{1,0:T(8,128)(2,1)}, u32[]{:S(2)}) %copy-start) | copy-done | bytes 524312
  3.6 1.0 %copy-done.1 = bf16[512,512]{1,0:T(8,128)(2,1)S(1)} copy-done((bf16[512,512]{1,0:T(8,128)(2,1)S(1)}, bf16[512,512]{1,0:T(8,128)(2,1)}, u32[]{:S(2)}) %copy-start.1) | copy-done | bytes 524312
  4.7 1.0 %copy-done.2 = bf16[512,512]{1,0:T(8,128)(2,1)S(1)} copy-done((bf16[512,512]{1,0:T(8,128)(2,1)S(1)}, bf16[512,512]{1,0:T(8,128)(2,1)}, u32[]{:S(2)}) %copy-start.2) | copy-done | bytes 524312
  5.7 1.0 %copy-done.3 = bf16[512,512]{1,0:T(8,128)(2,1)S(1)} copy-done((bf16[512,512]{1,0:T(8,128)(2,1)S(1)}, bf16[512,512]{1,0:T(8,128)(2,1)}, u32[]{:S(2)}) %copy-start.3) | copy-done | bytes 524312
  6.7 1.0 %copy-done.4 = bf16[512,512]{1,0:T(8,128)(2,1)S(1)} copy-done((bf16[512,512]{1,0:T(8,128)(2,1)S(1)}, bf16[512,512]{1,0:T(8,128)(2,1)}, u32[]{:S(2)}) %copy-start.4) | copy-done | bytes 524312
  7.8 1.0 %copy-done.5 = bf16[512,512]{1,0:T(8,128)(2,1)S(1)} copy-done((bf16[512,512]{1,0:T(8,128)(2,1)S(1)}, bf16[512,512]{1,0:T(8,128)(2,1)}, u32[]{:S(2)}) %copy-start.5) | copy-done | bytes 524312
  8.8 0.8 %copy-done.7 = bf16[64,512]{1,0:T(8,128)(2,1)S(1)} copy-done((bf16[64,512]{1,0:T(8,128)(2,1)S(1)}, bf16[64,512]{1,0:T(8,128)(2,1)}, u32[]{:S(2)}) %copy-start.7) | copy-done | bytes 65560
  9.7 0.8 %copy-done.8 = bf16[64,512]{1,0:T(8,128)(2,1)S(1)} copy-done((bf16[64,512]{1,0:T(8,128)(2,1)S(1)}, bf16[64,512]{1,0:T(8,128)(2,1)}, u32[]{:S(2)}) %copy-start.8) | copy-done | bytes 65560
  10.5 46.2 %shard_map.184 = (bf16[64,512]{1,0:T(8,128)(2,1)S(1)}, bf16[64,512]{1,0:T(8,128)(2,1)S(1)}, bf16[256,512]{1,0:T(8,128)(2,1)S(1)}) custom-call(bf16[256,512]{1,0:T(8,128)(2,1)S(1)} %copy-done.6, s32[256,1]{1,0:T(8,128)S(1)} %copy.20.band_ref, s32[256,2]{1,0:T(8,128)S(1)} %copy.21.rows_ref, bf16[64,512]{1,0:T(8,128)(2,1)S(1)} %copy-done.7, ...), custom_call_target="tpu_custom_call" | custom-call | tf_op jit(solution)/shard_map/pallas_call | solution.py:515
  56.7 0.6 %copy.26 = bf16[64,512]{1,0:T(8,128)(2,1)} copy(bf16[64,512]{1,0:T(8,128)(2,1)S(1)} %get-tuple-element.6) | data formatting | bytes 131072
  57.4 0.6 %copy.27 = bf16[64,512]{1,0:T(8,128)(2,1)} copy(bf16[64,512]{1,0:T(8,128)(2,1)S(1)} %get-tuple-element.7) | data formatting | bytes 131072
  58.0 0.7 %copy.28 = bf16[256,512]{1,0:T(8,128)(2,1)} copy(bf16[256,512]{1,0:T(8,128)(2,1)S(1)} %get-tuple-element.8) | data formatting | bytes 524288
  (13 shorter events, 0.0 us)
Async XLA Ops:
  0.6 0.8 %copy-start.14 = (s32[256,1]{0,1:T(1,128)S(1)}, s32[256,1]{0,1:T(1,128)}, u32[]{:S(2)}) copy-start(s32[256,1]{0,1:T(1,128)} %param.18) | copy-start | bytes 3076
  0.6 1.9 %copy-start.6 = (bf16[256,512]{1,0:T(8,128)(2,1)S(1)}, bf16[256,512]{1,0:T(8,128)(2,1)}, u32[]{:S(2)}) copy-start(bf16[256,512]{1,0:T(8,128)(2,1)} %grid_ref.1) | copy-start | bytes 786436
  1.6 0.9 %copy-start.9 = (s32[1,8,16]{2,1,0:T(8,128)S(1)}, s32[1,8,16]{2,1,0:T(8,128)}, u32[]{:S(2)}) copy-start(s32[1,8,16]{2,1,0:T(8,128)} %send_ref.1) | copy-start | bytes 1540
  1.6 0.9 %copy-start.10 = (f32[512]{0:T(512)S(1)}, f32[512]{0:T(512)}, u32[]{:S(2)}) copy-start(f32[512]{0:T(512)} %bias_grid_ref.1) | copy-start | bytes 6148
  1.6 0.9 %copy-start.11 = (f32[512]{0:T(512)S(1)}, f32[512]{0:T(512)}, u32[]{:S(2)}) copy-start(f32[512]{0:T(512)} %node_gain_ref.1) | copy-start | bytes 6148
  1.6 0.9 %copy-start.12 = (f32[512]{0:T(512)S(1)}, f32[512]{0:T(512)}, u32[]{:S(2)}) copy-start(f32[512]{0:T(512)} %bias_mesh_ref.1) | copy-start | bytes 6148
  1.7 0.9 %copy-start.13 = (f32[512]{0:T(512)S(1)}, f32[512]{0:T(512)}, u32[]{:S(2)}) copy-start(f32[512]{0:T(512)} %mesh_gain_ref.1) | copy-start | bytes 6148
  2.6 1.0 %copy-start = (bf16[512,512]{1,0:T(8,128)(2,1)S(1)}, bf16[512,512]{1,0:T(8,128)(2,1)}, u32[]{:S(2)}) copy-start(bf16[512,512]{1,0:T(8,128)(2,1)} %enc_send_hbm.1) | copy-start | bytes 1572868
  3.6 1.0 %copy-start.1 = (bf16[512,512]{1,0:T(8,128)(2,1)S(1)}, bf16[512,512]{1,0:T(8,128)(2,1)}, u32[]{:S(2)}) copy-start(bf16[512,512]{1,0:T(8,128)(2,1)} %enc_recv_hbm.1) | copy-start | bytes 1572868
  4.7 1.0 %copy-start.2 = (bf16[512,512]{1,0:T(8,128)(2,1)S(1)}, bf16[512,512]{1,0:T(8,128)(2,1)}, u32[]{:S(2)}) copy-start(bf16[512,512]{1,0:T(8,128)(2,1)} %enc_edge_hbm.1) | copy-start | bytes 1572868
  5.7 1.0 %copy-start.3 = (bf16[512,512]{1,0:T(8,128)(2,1)S(1)}, bf16[512,512]{1,0:T(8,128)(2,1)}, u32[]{:S(2)}) copy-start(bf16[512,512]{1,0:T(8,128)(2,1)} %proc_send_hbm.1) | copy-start | bytes 1572868
  6.7 1.0 %copy-start.4 = (bf16[512,512]{1,0:T(8,128)(2,1)S(1)}, bf16[512,512]{1,0:T(8,128)(2,1)}, u32[]{:S(2)}) copy-start(bf16[512,512]{1,0:T(8,128)(2,1)} %proc_recv_hbm.1) | copy-start | bytes 1572868
  7.8 1.0 %copy-start.5 = (bf16[512,512]{1,0:T(8,128)(2,1)S(1)}, bf16[512,512]{1,0:T(8,128)(2,1)}, u32[]{:S(2)}) copy-start(bf16[512,512]{1,0:T(8,128)(2,1)} %proc_edge_hbm.1) | copy-start | bytes 1572868
  8.8 0.8 %copy-start.7 = (bf16[64,512]{1,0:T(8,128)(2,1)S(1)}, bf16[64,512]{1,0:T(8,128)(2,1)}, u32[]{:S(2)}) copy-start(bf16[64,512]{1,0:T(8,128)(2,1)} %mesh_ref.1) | copy-start | bytes 196612
  9.7 0.8 %copy-start.8 = (bf16[64,512]{1,0:T(8,128)(2,1)S(1)}, bf16[64,512]{1,0:T(8,128)(2,1)}, u32[]{:S(2)}) copy-start(bf16[64,512]{1,0:T(8,128)(2,1)} %cot_ref.1) | copy-start | bytes 196612

commit v2 on v1

--- a/solution.py
+++ b/solution.py
@@ -54,6 +54,13 @@
     return jnp.sum(jnp.where(same, column, 0.0), 0, keepdims=True)
 
 
+def as_column(row):
+    n = row.shape[1]
+    shape = (n, n)
+    same = lax.broadcasted_iota(jnp.int32, shape, 0) == lax.broadcasted_iota(jnp.int32, shape, 1)
+    return jnp.sum(jnp.where(same, row, 0.0), 1, keepdims=True)
+
+
 def hot_rows(column, count):
     return (column == iota_f32((column.shape[0], count), 1)).astype(F32).astype(BF16)
 
@@ -65,32 +72,36 @@
 def kernel(
     bands,
     sectors,
+    *refs,
+):
+    inputs, outputs, local = refs[:17], refs[17:20], refs[20:37]
+    body(bands, sectors, inputs, *local, *outputs, *refs[37:])
+
+
+def body(
+    bands,
+    sectors,
+    inputs,
     grid_ref,
     band_ref,
     rows_ref,
     mesh_ref,
     slots_ref,
     send_ref,
-    enc_send_hbm,
-    enc_recv_hbm,
-    enc_edge_hbm,
+    enc_send,
+    enc_recv,
+    enc_edge,
     bias_grid_ref,
     node_gain_ref,
-    proc_send_hbm,
-    proc_recv_hbm,
-    proc_edge_hbm,
+    proc_send,
+    proc_recv,
+    proc_edge,
     bias_mesh_ref,
     mesh_gain_ref,
     cot_ref,
     mesh_out_ref,
     mesh_grad_ref,
     grid_grad_ref,
-    enc_send,
-    enc_recv,
-    enc_edge,
-    proc_send,
-    proc_recv,
-    proc_edge,
     slots_mine,
     slots_peer,
     gathered_mesh,
@@ -136,28 +147,28 @@
     lat, lon, sub = lax.axis_index("lat"), lax.axis_index("lon"), lax.axis_index("sub")
     other = 1 - sub
     nodes, width = grid_ref.shape
-    fanout = rows_ref.shape[1]
+    fanout = rows_ref.shape[0]
     mesh_rows = mesh_ref.shape[0]
     half = mesh_rows // 2
     half_all = bands * half
     bound = send_ref.shape[2]
-    edges_half = 2 * slots_ref.shape[1]
+    own_slots = slots_ref.shape[0]
+    edges_half = 2 * own_slots
     table_rows = table.shape[0]
 
-    weights = (
-        (enc_send_hbm, enc_send),
-        (enc_recv_hbm, enc_recv),
-        (enc_edge_hbm, enc_edge),
-        (proc_send_hbm, proc_send),
-        (proc_recv_hbm, proc_recv),
-        (proc_edge_hbm, proc_edge),
+    places = (
+        grid_ref, band_ref, rows_ref, mesh_ref, slots_ref, send_ref, enc_send, enc_recv, enc_edge,
+        bias_grid_ref, node_gain_ref, proc_send, proc_recv, proc_edge, bias_mesh_ref,
+        mesh_gain_ref, cot_ref,
     )
-    loads = [pltpu.make_async_copy(a, b, w_sem.at[n]) for n, (a, b) in enumerate(weights)]
-    for load in loads:
-        load.start()
+    loads = [
+        pltpu.make_async_copy(a, b, w_sem.at[n]) for n, (a, b) in enumerate(zip(inputs, places))
+    ]
+    early = (3, 4, 0, 6, 1, 2, 5)
+    for n in early + tuple(n for n in range(17) if n not in early):
+        loads[n].start()
 
     slots_mine[...] = jnp.zeros_like(slots_mine)
-    slots_mine[:, 0 : slots_ref.shape[1]] = slots_ref[...]
     table[mesh_rows:, :] = jnp.zeros((table_rows - mesh_rows, width), BF16)
     back_in[...] = jnp.zeros_like(back_in)
 
@@ -189,6 +200,9 @@
         def _():
             pl.semaphore_signal(barrier, inc=1, device_id=neighbour(d, 1), device_id_type=MESH)
     near = 2 + 2 * (lat > 0).astype(jnp.int32) + 2 * (lat < bands - 1).astype(jnp.int32)
+    loads[3].wait()
+    loads[4].wait()
+    slots_mine[0:own_slots, 0:mesh_rows] = slots_ref[...]
     pl.semaphore_wait(barrier, bands + near)
 
     def half_rows(which, band):
@@ -247,28 +261,27 @@
             copy.wait_recv()
         return onward
 
-    slot_copy = to_sub(slots_mine.at[peer_rows], slots_peer, 0)
+    slot_copy = to_sub(slots_mine, slots_peer, 0)
     slot_copy.start()
     gather_1 = gather_start(mesh_ref.at[my_rows], gathered_mesh, 0)
     gathered_mesh[half_rows(0, lat), :] = mesh_ref[0:half, :]
     gathered_mesh[half_rows(1, lat), :] = mesh_ref[half:, :]
 
+    for n in (0, 6, 9):
+        loads[n].wait()
     bias_grid = bias_grid_ref[...].reshape(1, width)
-    bias_mesh = bias_mesh_ref[...].reshape(1, width)
-    node_gain = node_gain_ref[...].reshape(1, width)
-    mesh_gain = mesh_gain_ref[...].reshape(1, width)
-
-    loads[0].wait()
-    proj_grid[...] = dot_plain(grid_ref[...], enc_send[...]).astype(BF16)
-
+    proj_grid[...] = (dot_plain(grid_ref[...], enc_send[...])).astype(BF16).astype(F32) + bias_grid
+
+    for n in (1, 2, 5):
+        loads[n].wait()
     band_of = band_ref[...]
     hots, hots_t = [], []
     for k in range(fanout):
-        row = rows_ref[:, k : k + 1]
+        row = rows_ref[k : k + 1, :]
         upper = (row >= half).astype(jnp.int32)
         place = (upper * (half_all - half) + band_of * half + row).astype(F32)
-        hots.append(hot_rows(place, 2 * half_all))
-        hots_t.append(hot_columns(as_row(place), 2 * half_all))
+        hots.append(hot_rows(as_column(place), 2 * half_all))
+        hots_t.append(hot_columns(place, 2 * half_all))
     hot_t = jnp.concatenate(hots_t, 1)
 
     listed = jnp.concatenate(
@@ -281,18 +294,23 @@
     pick_t = hot_columns(as_row(list_column), mesh_rows)
 
     slot_copy.wait()
-    own_slots = slots_ref[my_rows, :].astype(F32)
-    their_slots = slots_peer[...].astype(F32)
-    slot_column = jnp.concatenate(
-        [own_slots[:, k : k + 1] for k in range(edges_half // 2)]
-        + [their_slots[:, k : k + 1] for k in range(edges_half // 2)],
+    slot_lines = jnp.concatenate(
+        [
+            jnp.broadcast_to(ref[k : k + 1, :], (half, 128))
+            for ref in (slots_mine, slots_peer)
+            for k in range(own_slots)
+        ],
         0,
-    )
+    ).astype(F32)
+    shape = slot_lines.shape
+    lane = lax.broadcasted_iota(jnp.int32, shape, 1)
+    line = lax.rem(lax.broadcasted_iota(jnp.int32, shape, 0), half) + sub * half
+    slot_column = jnp.sum(jnp.where(lane == line, slot_lines, 0.0), 1, keepdims=True)
     slot_hot = hot_rows(slot_column, table_rows)
     slot_hot_t = hot_columns(as_row(slot_column), table_rows)
 
-    loads[1].wait()
-    loads[2].wait()
+    loads[7].wait()
+    loads[8].wait()
     onward_1 = gather_finish(gather_1, gathered_mesh, 0)
     proj_mesh = dot_plain(gathered_mesh[...], enc_recv[...]).astype(BF16)
     for k in range(fanout):
@@ -300,7 +318,7 @@
         pre_grid[base : base + nodes, :] = dot_plain(hots[k], proj_mesh)
         for at in range(0, nodes, CHUNK):
             here = slice(base + at, base + at + CHUNK)
-            pre = pre_grid[here, :] + proj_grid[at : at + CHUNK, :].astype(F32) + bias_grid
+            pre = pre_grid[here, :] + proj_grid[at : at + CHUNK, :]
             pre_grid[here, :] = pre
             hid[here, :] = (pre * jax.nn.sigmoid(pre)).astype(BF16)
         z_grid[base : base + nodes, :] = dot_plain(hid[base : base + nodes, :], enc_edge[...])
@@ -346,8 +364,11 @@
         hid[...], part_mine, part_out, part_in, lat_out, lat_in, 1, 1, lambda: None
     )
     slope_of(pre_grid, 0, fanout * nodes)
-    for n in range(3, 6):
+    for n in (10, 11, 12, 13, 14, 15, 16):
         loads[n].wait()
+    bias_mesh = bias_mesh_ref[...].reshape(1, width)
+    node_gain = node_gain_ref[...].reshape(1, width)
+    mesh_gain = mesh_gain_ref[...].reshape(1, width)
     agg_grid = scatter_finish(own, copies, lat_in)
 
     agg_grid_normed, agg_grid_inverse = norm_parts(agg_grid)
@@ -496,7 +517,21 @@
     mesh_grad_ref[peer_rows, :] = grad_half_peer[...]
 
 
+def store_kernel(a, b, c, a_out, b_out, c_out, sems):
+    copies = [
+        pltpu.make_async_copy(source, target, sems.at[n])
+        for n, (source, target) in enumerate(((a, a_out), (b, b_out), (c, c_out)))
+    ]
+    for copy in copies:
+        copy.start()
+    for copy in copies:
+        copy.wait()
+
+
 def on_device(bands, sectors, *args):
+    args = list(args)
+    for n in (1, 2, 4):
+        args[n] = args[n].T
     grid_latent, mesh_latent, mesh_slots = args[0], args[3], args[4]
     send_rows, edge_rows = args[5], args[2]
     nodes, width = grid_latent.shape
@@ -504,29 +539,29 @@
     half = mesh_rows // 2
     bound = 8 * send_rows.shape[2]
     table_rows = -(-(mesh_rows + bound) // 128) * 128
-    edges = edge_rows.shape[1] * nodes
-    mesh_edges = 2 * mesh_slots.shape[1] * half
+    edges = edge_rows.shape[0] * nodes
+    mesh_edges = 2 * mesh_slots.shape[0] * half
     every = bands * mesh_rows
     most = max(edges, mesh_edges)
     vmem = pl.BlockSpec(memory_space=pltpu.VMEM)
-    hbm = pl.BlockSpec(memory_space=pl.ANY)
-    weights = (6, 7, 8, 11, 12, 13)
+    hbm = pl.BlockSpec(memory_space=pltpu.HBM)
     dma = pltpu.SemaphoreType.DMA
-    return pl.pallas_call(
+    out_shape = (
+        jax.ShapeDtypeStruct((mesh_rows, width), BF16),
+        jax.ShapeDtypeStruct((mesh_rows, width), BF16),
+        jax.ShapeDtypeStruct((nodes, width), BF16),
+    )
+    results = pl.pallas_call(
         functools.partial(kernel, bands, sectors),
-        out_shape=(
-            jax.ShapeDtypeStruct((mesh_rows, width), BF16),
-            jax.ShapeDtypeStruct((mesh_rows, width), BF16),
-            jax.ShapeDtypeStruct((nodes, width), BF16),
-        ),
-        in_specs=[hbm if n in weights else vmem for n in range(len(args))],
+        out_shape=out_shape,
+        in_specs=[hbm] * len(args),
         out_specs=(vmem, vmem, vmem),
-        scratch_shapes=[pltpu.VMEM((width, width), BF16)] * 6
+        scratch_shapes=[pltpu.VMEM(a.shape, a.dtype) for a in args]
         + [
-            pltpu.VMEM((mesh_rows, 128), jnp.int32),
-            pltpu.VMEM((half, 128), jnp.int32),
+            pltpu.VMEM((8, 128), jnp.int32),
+            pltpu.VMEM((8, 128), jnp.int32),
             pltpu.VMEM((every, width), BF16),
-            pltpu.VMEM((nodes, width), BF16),
+            pltpu.VMEM((nodes, width), F32),
             pltpu.VMEM((edges, width), F32),
             pltpu.VMEM((edges, width), F32),
             pltpu.VMEM((edges, 1), F32),
@@ -555,7 +590,7 @@
             pltpu.VMEM((bands, half, width), BF16),
             pltpu.VMEM((half, width), BF16),
             pltpu.VMEM((half, width), BF16),
-            dma((6,)),
+            dma((17,)),
             dma((4, bands)),
             dma((4, bands)),
             dma((2, bands)),
@@ -566,9 +601,16 @@
             dma((2, 8)),
         ],
         compiler_params=pltpu.CompilerParams(
-            collective_id=0, has_side_effects=True, vmem_limit_bytes=48 * 1024 * 1024
+            collective_id=0, has_side_effects=True, vmem_limit_bytes=63 * 1024 * 1024 + 512 * 1024
         ),
     )(*args)
+    return pl.pallas_call(
+        store_kernel,
+        out_shape=out_shape,
+        in_specs=[vmem] * 3,
+        out_specs=[hbm] * 3,
+        scratch_shapes=[dma((3,))],
+    )(*results)
 
 
 def solution(mesh):

time: 59.2 us -> 49.5 us (0.84)
  local copies, waits for them, and re-layouts: 11.7 us -> 0 us
  Pallas kernels: 46.2 us -> 48.7 us
    unnamed x36 -> x0, local copies, waits for them, and re-layouts: 11.7 us -> none
    pallas_call x1 -> x2, Pallas kernels: 46.2 us -> 48.7 us  [the longest x1 46.9 us: on_device(): pl.pallas_call(functools.partial(kernel, bands, sectors), out_shape=out_s...]
where the time goes in v2:
time: 49.5 us; the launch traced here: 49.4 us
  Pallas kernels  48.7 us (98%)
  between operations  0.65 us (1%)
    pallas_call x1, Pallas kernels, on_device(): pl.pallas_call(functools.partial(kernel, bands, sectors), out_shape=out_s...  46.9 us
    pallas_call x1, Pallas kernels, on_device(): pl.pallas_call(store_kernel, out_shape=out_shape, in_specs=[vmem] * 3, ou...  1.8 us

profile of v2, /device:TPU:0, one launch (start us, length us, event | category | flops | bytes accessed | tf_op | source)
XLA Modules:
  0.0 49.4 jit_solution(15977302871063288953)
XLA Ops:
  0.6 46.9 %shard_map.184 = (bf16[64,512]{1,0:T(8,128)(2,1)}, bf16[64,512]{1,0:T(8,128)(2,1)}, bf16[256,512]{1,0:T(8,128)(2,1)}) custom-call(bf16[256,512]{1,0:T(8,128)(2,1)} %refs_0_.1, s32[1,256]{1,0:T(1,128)} %bitcast.5, s32[2,256]{1,0:T(2,128)} %bitcast.3, bf16[64,512]{1,0:T(8,128)(2,1)} %refs_3_.1, s32[4,64]{1,0:T(4,128)} %bitcast.4, s32[1,8,16]{2,1,0:T(8,128)} %refs_5_.1, ...), custom_call_target="tpu_custom_call" | custom-call | tf_op jit(solution)/shard_map/pallas_call | solution.py:554
  47.6 1.8 %shard_map.185 = (bf16[64,512]{1,0:T(8,128)(2,1)}, bf16[64,512]{1,0:T(8,128)(2,1)}, bf16[256,512]{1,0:T(8,128)(2,1)}) custom-call(bf16[64,512]{1,0:T(8,128)(2,1)} %get-tuple-element.6.a, bf16[64,512]{1,0:T(8,128)(2,1)} %get-tuple-element.7.b, bf16[256,512]{1,0:T(8,128)(2,1)} %get-tuple-element.8.c), custom_call_target="tpu_custom_call" | custom-call | tf_op jit(solution)/shard_map/pallas_call | solution.py:607

commit v3 on v2

--- a/solution.py
+++ b/solution.py
@@ -9,6 +9,7 @@
 
 EPS = 1e-05
 DIRECTIONS = ((-1, -1), (-1, 0), (-1, 1), (0, -1), (0, 1), (1, -1), (1, 0), (1, 1))
+ORDER = (0, 2, 1, 3, 4, 5, 7, 6)
 MESH = pl.DeviceIdType.MESH
 F32 = jnp.float32
 BF16 = jnp.bfloat16
@@ -74,14 +75,15 @@
     sectors,
     *refs,
 ):
-    inputs, outputs, local = refs[:17], refs[17:20], refs[20:37]
-    body(bands, sectors, inputs, *local, *outputs, *refs[37:])
+    inputs, outputs, local = refs[:17], refs[17:20], refs[20:40]
+    body(bands, sectors, inputs, outputs, *local, *refs[40:])
 
 
 def body(
     bands,
     sectors,
     inputs,
+    outputs,
     grid_ref,
     band_ref,
     rows_ref,
@@ -143,6 +145,9 @@
     sub_r,
     nb_s,
     nb_r,
+    hot_t,
+    chunk_s,
+    chunk_r,
 ):
     lat, lon, sub = lax.axis_index("lat"), lax.axis_index("lon"), lax.axis_index("sub")
     other = 1 - sub
@@ -156,6 +161,38 @@
     edges_half = 2 * own_slots
     table_rows = table.shape[0]
 
+    slots_mine[...] = jnp.zeros_like(slots_mine)
+    table[mesh_rows:, :] = jnp.zeros((table_rows - mesh_rows, width), BF16)
+    back_in[...] = jnp.zeros_like(back_in)
+
+    barrier = pltpu.get_barrier_semaphore()
+
+    def lat_peer(step):
+        return lax.rem(lat + step, bands)
+
+    def reaches(d):
+        target = lat + DIRECTIONS[d][0]
+        return (target >= 0) & (target < bands)
+
+    def comes_from(d):
+        target = lat - DIRECTIONS[d][0]
+        return (target >= 0) & (target < bands)
+
+    def neighbour(d, sign):
+        return {
+            "lat": lat + sign * DIRECTIONS[d][0],
+            "lon": lax.rem(lon + sign * DIRECTIONS[d][1] + sectors, sectors),
+        }
+
+    for step in range(1, bands):
+        pl.semaphore_signal(barrier, inc=1, device_id={"lat": lat_peer(step)}, device_id_type=MESH)
+    pl.semaphore_signal(barrier, inc=1, device_id={"sub": other}, device_id_type=MESH)
+    diagonal = [d for d in range(8) if DIRECTIONS[d][1] != 0]
+    for d in diagonal:
+        @pl.when(reaches(d))
+        def _():
+            pl.semaphore_signal(barrier, inc=1, device_id=neighbour(d, 1), device_id_type=MESH)
+
     places = (
         grid_ref, band_ref, rows_ref, mesh_ref, slots_ref, send_ref, enc_send, enc_recv, enc_edge,
         bias_grid_ref, node_gain_ref, proc_send, proc_recv, proc_edge, bias_mesh_ref,
@@ -168,37 +205,10 @@
     for n in early + tuple(n for n in range(17) if n not in early):
         loads[n].start()
 
-    slots_mine[...] = jnp.zeros_like(slots_mine)
-    table[mesh_rows:, :] = jnp.zeros((table_rows - mesh_rows, width), BF16)
-    back_in[...] = jnp.zeros_like(back_in)
-
-    barrier = pltpu.get_barrier_semaphore()
-
-    def lat_peer(step):
-        return lax.rem(lat + step, bands)
-
-    def reaches(d):
-        target = lat + DIRECTIONS[d][0]
-        return (target >= 0) & (target < bands)
-
-    def comes_from(d):
-        target = lat - DIRECTIONS[d][0]
-        return (target >= 0) & (target < bands)
-
-    def neighbour(d, sign):
-        return {
-            "lat": lat + sign * DIRECTIONS[d][0],
-            "lon": lax.rem(lon + sign * DIRECTIONS[d][1] + sectors, sectors),
-        }
-
-    for step in range(1, bands):
-        pl.semaphore_signal(barrier, inc=1, device_id={"lat": lat_peer(step)}, device_id_type=MESH)
-    pl.semaphore_signal(barrier, inc=1, device_id={"sub": other}, device_id_type=MESH)
-    diagonal = [d for d in range(8) if DIRECTIONS[d][1] != 0]
-    for d in diagonal:
-        @pl.when(reaches(d))
-        def _():
-            pl.semaphore_signal(barrier, inc=1, device_id=neighbour(d, 1), device_id_type=MESH)
+    stores = [
+        pltpu.make_async_copy(a, b, w_sem.at[17 + n])
+        for n, (a, b) in enumerate(zip((mesh_out_ref, mesh_grad_ref, grid_grad_ref), outputs))
+    ]
     near = 2 + 2 * (lat > 0).astype(jnp.int32) + 2 * (lat < bands - 1).astype(jnp.int32)
     loads[3].wait()
     loads[4].wait()
@@ -210,6 +220,9 @@
 
     def band_rows(band):
         return pl.ds(pl.multiple_of(band * half, half), half)
+
+    def all_half(which):
+        return pl.ds(pl.multiple_of(which * half_all, half_all), half_all)
 
     my_rows = pl.ds(pl.multiple_of(sub * half, half), half)
     peer_rows = pl.ds(pl.multiple_of(other * half, half), half)
@@ -282,10 +295,10 @@
         place = (upper * (half_all - half) + band_of * half + row).astype(F32)
         hots.append(hot_rows(as_column(place), 2 * half_all))
         hots_t.append(hot_columns(place, 2 * half_all))
-    hot_t = jnp.concatenate(hots_t, 1)
+    hot_t[...] = jnp.concatenate(hots_t, 1)
 
     listed = jnp.concatenate(
-        [jnp.broadcast_to(send_ref[0, d : d + 1, :], (bound, bound)) for d in range(8)], 0
+        [jnp.broadcast_to(send_ref[0, d : d + 1, :], (bound, bound)) for d in ORDER], 0
     ).astype(F32)
     lane = lax.broadcasted_iota(jnp.int32, (8 * bound, bound), 1)
     line = lax.rem(lax.broadcasted_iota(jnp.int32, (8 * bound, bound), 0), bound)
@@ -305,7 +318,11 @@
     shape = slot_lines.shape
     lane = lax.broadcasted_iota(jnp.int32, shape, 1)
     line = lax.rem(lax.broadcasted_iota(jnp.int32, shape, 0), half) + sub * half
-    slot_column = jnp.sum(jnp.where(lane == line, slot_lines, 0.0), 1, keepdims=True)
+    slot_raw = slot_column = jnp.sum(jnp.where(lane == line, slot_lines, 0.0), 1, keepdims=True)
+    for d, move in ((1, bound), (2, -bound), (6, bound), (7, -bound)):
+        first = mesh_rows + d * bound
+        inside = (slot_raw >= first) & (slot_raw < first + bound)
+        slot_column = slot_column + jnp.where(inside, float(move), 0.0)
     slot_hot = hot_rows(slot_column, table_rows)
     slot_hot_t = hot_columns(as_row(slot_column), table_rows)
 
@@ -329,17 +346,28 @@
             inv_grid[here, :] = inverse
             hid[here, :] = normed.astype(BF16)
 
-    def scatter_sum(values, mine, out, inbound, out_lat, in_lat, n_sub, n_lat, meanwhile):
-        total = dot_plain(hot_t, values)
-        low, high = total[0:half_all, :], total[half_all:, :]
-        out[...] = jnp.where(sub == 0, high, low).astype(BF16)
-        copy = to_sub(out, inbound, n_sub)
-        copy.start()
-        mine[...] = jnp.where(sub == 0, low, high)
-        meanwhile()
-        copy.wait()
+    def scatter_sum(values, mine, out, inbound, out_lat, in_lat, n_sub, n_lat):
+        out[...] = dot_plain(hot_t[all_half(other), :], values).astype(BF16)
+        order = list(range(1, bands)) + [0]
+        across = []
+        for step in order:
+            rows = band_rows(lat_peer(step))
+            copy = pltpu.make_async_remote_copy(
+                src_ref=out.at[rows],
+                dst_ref=inbound.at[rows],
+                send_sem=chunk_s.at[n_sub, step],
+                recv_sem=chunk_r.at[n_sub, step],
+                device_id={"sub": other},
+                device_id_type=MESH,
+            )
+            copy.start()
+            across.append(copy)
+        mine[...] = dot_plain(hot_t[all_half(sub), :], values)
         copies = []
-        for step in range(bands - 1, 0, -1):
+        for copy, step in zip(across, order):
+            copy.wait()
+            if step == 0:
+                continue
             rows = band_rows(lat_peer(step))
             out_lat[rows, :] = (mine[rows, :] + inbound[rows, :].astype(F32)).astype(BF16)
             copy = to_lat(out_lat.at[rows], in_lat.at[step], n_lat, step)
@@ -361,7 +389,7 @@
             ref[at : at + CHUNK, :] = silu_slope(ref[at : at + CHUNK, :])
 
     own, copies = scatter_sum(
-        hid[...], part_mine, part_out, part_in, lat_out, lat_in, 1, 1, lambda: None
+        hid[...], part_mine, part_out, part_in, lat_out, lat_in, 0, 1
     )
     slope_of(pre_grid, 0, fanout * nodes)
     for n in (10, 11, 12, 13, 14, 15, 16):
@@ -381,31 +409,36 @@
     send_mesh = dot_plain(mid_full[...], proc_send[...]).astype(BF16)
     bound_out[...] = dot_plain(pick, send_mesh).astype(BF16)
 
-    def block_of(d):
-        return pl.ds(d * bound, bound)
-
-    def table_of(d):
-        return pl.ds(mesh_rows + d * bound, bound)
-
-    def to_near(source, target, n, d, sign):
+    if sectors == 2:
+        runs = ((0, 2), (2, 1), (3, 2), (5, 2), (7, 1))
+    else:
+        runs = tuple((at, 1) for at in range(8))
+
+    def block_of(run):
+        return pl.ds(run[0] * bound, run[1] * bound)
+
+    def table_of(run):
+        return pl.ds(mesh_rows + run[0] * bound, run[1] * bound)
+
+    def to_near(source, target, n, run, sign):
         return pltpu.make_async_remote_copy(
             src_ref=source,
             dst_ref=target,
-            send_sem=nb_s.at[n, d],
-            recv_sem=nb_r.at[n, d],
-            device_id=neighbour(d, sign),
+            send_sem=nb_s.at[n, run[0]],
+            recv_sem=nb_r.at[n, run[0]],
+            device_id=neighbour(ORDER[run[0]], sign),
             device_id_type=MESH,
         )
 
-    for d in range(8):
-        @pl.when(reaches(d))
+    for d in runs:
+        @pl.when(reaches(ORDER[d[0]]))
         def _():
             to_near(bound_out.at[block_of(d)], table.at[table_of(d)], 0, d, 1).start()
     table[0:mesh_rows, :] = send_mesh
-    for d in range(8):
+    for d in runs:
         copy = to_near(bound_out.at[block_of(d)], table.at[table_of(d)], 0, d, 1)
 
-        @pl.when(comes_from(d))
+        @pl.when(comes_from(ORDER[d[0]]))
         def _():
             copy.wait_recv()
 
@@ -447,15 +480,15 @@
         d_recv = d_recv + d_pre.astype(F32)
     d_table = dot_plain(slot_hot_t, hid[0:edges, :])
     back_out[...] = d_table[mesh_rows : mesh_rows + 8 * bound, :].astype(BF16)
-    for d in range(8):
-        @pl.when(comes_from(d))
+    for d in runs:
+        @pl.when(comes_from(ORDER[d[0]]))
         def _():
             to_near(back_out.at[block_of(d)], back_in.at[block_of(d)], 1, d, -1).start()
     d_mid = upstream + dot_trans(d_recv.astype(BF16), proc_recv[...])
-    for d in range(8):
+    for d in runs:
         copy = to_near(back_out.at[block_of(d)], back_in.at[block_of(d)], 1, d, -1)
 
-        @pl.when(reaches(d))
+        @pl.when(reaches(ORDER[d[0]]))
         def _():
             copy.wait_recv()
     d_send = d_table[0:mesh_rows, :] + dot_plain(pick_t, back_in[...])
@@ -473,6 +506,7 @@
     gather_2 = gather_start(d_agg_all.at[half_rows(sub, lat)], d_agg_all, 2)
     out_copy.wait()
     mesh_out_ref[peer_rows, :] = out_half_peer[...]
+    stores[0].start()
     onward_2 = gather_finish(gather_2, d_agg_all, 1)
     own_copy.wait()
 
@@ -492,9 +526,10 @@
         for k in range(1, fanout):
             total = total + hid[k * nodes : (k + 1) * nodes, :].astype(F32)
         grid_grad_ref[...] = dot_trans(total.astype(BF16), enc_send[...]).astype(BF16)
+        stores[2].start()
 
     own, copies_2 = scatter_sum(
-        hid[...], part_mine, part_out_2, part_in_2, lat_out_2, lat_in_2, 6, 3, lambda: None
+        hid[...], part_mine, part_out_2, part_in_2, lat_out_2, lat_in_2, 1, 3
     )
     grid_side()
     d_proj_mesh = scatter_finish(own, copies_2, lat_in_2)
@@ -505,16 +540,19 @@
     mesh_grad_ref[my_rows, :] = grad_half
     for copy in gather_1 + gather_2 + onward_1 + onward_2:
         copy.wait_send()
-    for d in range(8):
-        @pl.when(reaches(d))
+    for d in runs:
+        @pl.when(reaches(ORDER[d[0]]))
         def _():
             to_near(bound_out.at[block_of(d)], table.at[table_of(d)], 0, d, 1).wait_send()
 
-        @pl.when(comes_from(d))
+        @pl.when(comes_from(ORDER[d[0]]))
         def _():
             to_near(back_out.at[block_of(d)], back_in.at[block_of(d)], 1, d, -1).wait_send()
     grad_copy.wait()
     mesh_grad_ref[peer_rows, :] = grad_half_peer[...]
+    stores[1].start()
+    for store in stores:
+        store.wait()
 
 
 def store_kernel(a, b, c, a_out, b_out, c_out, sems):
@@ -543,7 +581,6 @@
     mesh_edges = 2 * mesh_slots.shape[0] * half
     every = bands * mesh_rows
     most = max(edges, mesh_edges)
-    vmem = pl.BlockSpec(memory_space=pltpu.VMEM)
     hbm = pl.BlockSpec(memory_space=pltpu.HBM)
     dma = pltpu.SemaphoreType.DMA
     out_shape = (
@@ -555,8 +592,8 @@
         functools.partial(kernel, bands, sectors),
         out_shape=out_shape,
         in_specs=[hbm] * len(args),
-        out_specs=(vmem, vmem, vmem),
-        scratch_shapes=[pltpu.VMEM(a.shape, a.dtype) for a in args]
+        out_specs=(hbm, hbm, hbm),
+        scratch_shapes=[pltpu.VMEM(a.shape, a.dtype) for a in (*args, *out_shape)]
         + [
             pltpu.VMEM((8, 128), jnp.int32),
             pltpu.VMEM((8, 128), jnp.int32),
@@ -590,7 +627,7 @@
             pltpu.VMEM((bands, half, width), BF16),
             pltpu.VMEM((half, width), BF16),
             pltpu.VMEM((half, width), BF16),
-            dma((17,)),
+            dma((20,)),
             dma((4, bands)),
             dma((4, bands)),
             dma((2, bands)),
@@ -599,6 +636,9 @@
             dma((8,)),
             dma((2, 8)),
             dma((2, 8)),
+            pltpu.VMEM((every, edges), BF16),
+            dma((2, bands)),
+            dma((2, bands)),
         ],
         compiler_params=pltpu.CompilerParams(
             collective_id=0, has_side_effects=True, vmem_limit_bytes=63 * 1024 * 1024 + 512 * 1024
@@ -607,7 +647,7 @@
     return pl.pallas_call(
         store_kernel,
         out_shape=out_shape,
-        in_specs=[vmem] * 3,
+        in_specs=[pl.BlockSpec(memory_space=pltpu.VMEM)] * 3,
         out_specs=[hbm] * 3,
         scratch_shapes=[dma((3,))],
     )(*results)

time: 49.5 us -> 47.7 us (0.964)
  Pallas kernels: 48.7 us -> 46.9 us
    pallas_call x1, Pallas kernels: 46.9 us -> 45.1 us  [on_device(): pl.pallas_call(functools.partial(kernel, bands, sectors), out_shape=out_s...]
where the time goes in v3:
time: 47.7 us; the launch traced here: 47.6 us
  Pallas kernels  46.9 us (98%)
  between operations  0.65 us (1%)
    pallas_call x1, Pallas kernels, on_device(): pl.pallas_call(functools.partial(kernel, bands, sectors), out_shape=out_s...  45.1 us
    pallas_call x1, Pallas kernels, on_device(): pl.pallas_call(store_kernel, out_shape=out_shape, in_specs=[pl.BlockSpec(...  1.8 us

profile of v3, /device:TPU:0, one launch (start us, length us, event | category | flops | bytes accessed | tf_op | source)
XLA Modules:
  0.0 47.6 jit_solution(6192499859708075121)
XLA Ops:
  0.6 45.1 %shard_map.184 = (bf16[64,512]{1,0:T(8,128)(2,1)}, bf16[64,512]{1,0:T(8,128)(2,1)}, bf16[256,512]{1,0:T(8,128)(2,1)}) custom-call(bf16[256,512]{1,0:T(8,128)(2,1)} %refs_0_.1, s32[1,256]{1,0:T(1,128)} %bitcast.5, s32[2,256]{1,0:T(2,128)} %bitcast.3, bf16[64,512]{1,0:T(8,128)(2,1)} %refs_3_.1, s32[4,64]{1,0:T(4,128)} %bitcast.4, s32[1,8,16]{2,1,0:T(8,128)} %refs_5_.1, ...), custom_call_target="tpu_custom_call" | custom-call | tf_op jit(solution)/shard_map/pallas_call | solution.py:591
  45.8 1.8 %shard_map.185 = (bf16[64,512]{1,0:T(8,128)(2,1)}, bf16[64,512]{1,0:T(8,128)(2,1)}, bf16[256,512]{1,0:T(8,128)(2,1)}) custom-call(bf16[64,512]{1,0:T(8,128)(2,1)} %get-tuple-element.6.a, bf16[64,512]{1,0:T(8,128)(2,1)} %get-tuple-element.7.b, bf16[256,512]{1,0:T(8,128)(2,1)} %get-tuple-element.8.c), custom_call_target="tpu_custom_call" | custom-call | tf_op jit(solution)/shard_map/pallas_call | solution.py:647
